TPU v7x, 32 devices: a whole 2x2x4 slice. The times are simulated.
32 devices in a mesh: groups: 2 (over y), ctx: 4 (over z), fsdp: 2 (over x), sub: 2 (over core).
Axes of the slice: x: 2, y: 2, z: 4, core: 2. Of those that a mesh axis runs over, the one named last changes fastest.
Arguments:
- streams: bfloat16 [3, 2048, 4096], P(None, ('groups', 'ctx', 'sub'), 'fsdp'), parts along dimension 1, may hold values from -6 to 6
- feat_taps: float32 [3, 7, 4096], P(None, None, 'fsdp'), may hold values from -2.4 to 2.4
- long_filter: bfloat16 [128, 4096], P('ctx', 'fsdp'), may hold values from -0.5 to 0.5
- upstream: bfloat16 [2048, 4096], P(('groups', 'ctx', 'sub'), 'fsdp'), parts along dimension 0, may hold values from -6 to 6
- score_dir: float32 [4096], P('fsdp'), may hold values from -21 to 21
- seg_lengths: int32 [16], P('groups'), parts along dimension 0, may hold values from 1 to 512, 1024 in all
- list_ids: int32 [16], P('groups'), parts along dimension 0, may hold values from 0 to 1
Outputs:
- d_streams: bfloat16 [3, 2048, 4096], P(None, ('groups', 'ctx', 'sub'), 'fsdp'), parts along dimension 1
- d_feat: float32 [6, 7, 4096], P('groups', None, 'fsdp'), parts along dimension 0
- d_filter: float32 [256, 4096], P(('groups', 'ctx'), 'fsdp'), parts along dimension 0
There are 2 independent parts, one for each index of `groups`. A program takes and returns all parts, laid end to end along the dimension named above; an argument that names none is the same for every part. Nothing has to cross between parts.
Inputs may be any that keep to these rules, and one draw needn't show every extreme that they name: `seg_lengths`: the lengths sum to 1024 and the longest segment has exactly 512 tokens.
All inputs are finite; a program needn't handle non-finite values.
Results may differ from a plain program's by a relative error of at most 0.012.
Values may be sent and summed in bfloat16 or wider, within the bound.
No kernel may reach another device: no remote copies, remote signals or barrier semaphores. Data moves between devices by JAX's collectives and lax.ppermute only.
A program may use at most 64 MiB of HBM per device.

v0:
```python
import jax
import jax.numpy as jnp
from jax import lax
from jax.sharding import PartitionSpec as P

LH = 128
KF = 7


HIGH = lax.Precision.HIGHEST


def passed_along(value, axis, steps):
    count = lax.axis_size(axis)
    leading, last = (max(0, -steps), min(count, count - steps))
    return lax.ppermute(value, axis, [(source, source + steps) for source in range(leading, last)])


def tap_block(tap_count):
    return 16 if tap_count % 16 == 0 else tap_count


def segment_age(seg_lengths, positions):
    offsets = jnp.cumsum(seg_lengths, dtype=jnp.int32) - seg_lengths
    member = offsets[None, :] <= positions[:, None]
    seg_index = jnp.sum(member.astype(jnp.int32), axis=1, dtype=jnp.int32) - 1
    seg_start = jnp.max(jnp.where(member, offsets[None, :], 0), axis=1)
    return (seg_index, positions - seg_start)


def causal_taps(tap_table, extended, row_age, tok_rows):
    tap_count = tap_table.shape[0]
    per_turn = tap_block(tap_count)

    def causal_advance(b, running):
        for m in range(per_turn):
            j = b * per_turn + m
            window = lax.dynamic_slice_in_dim(extended, tap_count - 1 - j, tok_rows, 0)
            weight_row = lax.dynamic_index_in_dim(tap_table, j, 0, keepdims=False)
            running = running + jnp.where(
                (row_age >= j)[:, None], weight_row[None, :] * window.astype(jnp.float32), 0.0
            )
        return running

    start_sum = jnp.zeros((tok_rows, extended.shape[1]), jnp.float32)
    return lax.fori_loop(0, tap_count // per_turn, causal_advance, start_sum)


def reverse_taps(tap_table, extended, ext_age, tok_rows):
    tap_count = tap_table.shape[0]
    per_turn = tap_block(tap_count)

    def reverse_advance(b, running):
        for m in range(per_turn):
            j = b * per_turn + m
            window = lax.dynamic_slice_in_dim(extended, j, tok_rows, 0)
            keep = lax.dynamic_slice_in_dim(ext_age, j, tok_rows, 0) >= j
            weight_row = lax.dynamic_index_in_dim(tap_table, j, 0, keepdims=False)
            running = running + jnp.where(
                keep[:, None], weight_row[None, :] * window.astype(jnp.float32), 0.0
            )
        return running

    start_sum = jnp.zeros((tok_rows, extended.shape[1]), jnp.float32)
    return lax.fori_loop(0, tap_count // per_turn, reverse_advance, start_sum)


def correlate_taps(gradient, extended, row_age, tap_count, tok_rows):
    per_turn = tap_block(tap_count)

    def correlate_advance(b, result):
        collected = []
        for m in range(per_turn):
            j = b * per_turn + m
            window = lax.dynamic_slice_in_dim(extended, tap_count - 1 - j, tok_rows, 0)
            product = gradient.astype(jnp.float32) * window.astype(jnp.float32)
            collected.append(jnp.sum(jnp.where((row_age >= j)[:, None], product, 0.0), axis=0))
        return lax.dynamic_update_slice_in_dim(result, jnp.stack(collected), b * per_turn, 0)

    start_rows = jnp.zeros((tap_count, gradient.shape[1]), jnp.float32)
    return lax.fori_loop(0, tap_count // per_turn, correlate_advance, start_rows)


def list_coef(totals, seg_lengths, list_ids):
    length_f = seg_lengths.astype(jnp.float32)
    scores = totals / length_f
    mates = (list_ids[:, None] == list_ids[None, :]).astype(jnp.float32)
    mean_score = jnp.dot(mates, scores, precision=HIGH) / jnp.sum(mates, axis=1)
    return (scores - mean_score) / length_f


def local(streams, feat_taps, long_filter, upstream, score_dir, seg_lengths, list_ids):
    tok_rows = streams.shape[1]
    seg_count = seg_lengths.shape[0]
    first_row = lax.axis_index(("ctx", "sub")) * tok_rows
    positions = first_row + jnp.arange(tok_rows + LH - 1, dtype=jnp.int32)
    seg_span, age_span = segment_age(seg_lengths, positions)
    seg_index = seg_span[:tok_rows]
    row_age = age_span[:tok_rows]
    left_rim = passed_along(streams[:, tok_rows - (KF - 1) :, :], ("ctx", "sub"), 1)
    stream_ext = jnp.concatenate([left_rim, streams], axis=1)
    featured = [
        causal_taps(feat_taps[i], stream_ext[i], row_age, tok_rows).astype(jnp.bfloat16)
        for i in range(3)
    ]
    query, key_feat, value_feat = featured
    product = (key_feat.astype(jnp.float32) * value_feat.astype(jnp.float32)).astype(jnp.bfloat16)
    filt = lax.all_gather(long_filter, "ctx", axis=0, tiled=True).astype(jnp.float32)
    prod_rim = passed_along(product[tok_rows - (LH - 1) :], ("ctx", "sub"), 1)
    prod_ext = jnp.concatenate([prod_rim, product], axis=0)
    mixed = causal_taps(filt, prod_ext, row_age, tok_rows)
    out_y = query.astype(jnp.float32) * mixed
    projected = jnp.dot(out_y, score_dir, precision=HIGH)
    onehot = (seg_index[:, None] == jnp.arange(seg_count, dtype=jnp.int32)[None, :]).astype(
        jnp.float32
    )
    partial_sums = jnp.dot(projected, onehot, precision=HIGH)
    totals = lax.psum(partial_sums, ("ctx", "fsdp", "sub"))
    coef = list_coef(totals, seg_lengths, list_ids)
    tok_coef = jnp.dot(onehot, coef, precision=HIGH)
    d_out = upstream.astype(jnp.float32) + tok_coef[:, None] * score_dir[None, :]
    d_query = (d_out * mixed).astype(jnp.bfloat16)
    d_mixed = (d_out * query.astype(jnp.float32)).astype(jnp.bfloat16)
    grad_rim = passed_along(d_mixed[: LH - 1], ("ctx", "sub"), -1)
    dm_ext = jnp.concatenate([d_mixed, grad_rim], axis=0)
    d_prod = reverse_taps(filt, dm_ext, age_span, tok_rows)
    d_key = (d_prod * value_feat.astype(jnp.float32)).astype(jnp.bfloat16)
    d_value = (d_prod * key_feat.astype(jnp.float32)).astype(jnp.bfloat16)
    filter_part = correlate_taps(d_mixed, prod_ext, row_age, LH, tok_rows)
    grads = jnp.stack([d_query, d_key, d_value])
    feat_rim = passed_along(grads[:, : KF - 1, :], ("ctx", "sub"), -1)
    grads_ext = jnp.concatenate([grads, feat_rim], axis=1)
    d_streams = jnp.stack(
        [reverse_taps(feat_taps[i], grads_ext[i], age_span, tok_rows) for i in range(3)]
    ).astype(jnp.bfloat16)
    taps_part = jnp.stack(
        [correlate_taps(grads[i], stream_ext[i], row_age, KF, tok_rows) for i in range(3)]
    )
    shard_rows = long_filter.shape[0]
    filter_all, d_feat = lax.psum((filter_part, taps_part), ("ctx", "sub"))
    d_filter = lax.dynamic_slice_in_dim(
        filter_all, lax.axis_index("ctx") * shard_rows, shard_rows, 0
    )
    return (d_streams, d_feat, d_filter)


def solution(mesh):
    placed = (
        P(None, ("groups", "ctx", "sub"), "fsdp"),
        P(None, None, "fsdp"),
        P("ctx", "fsdp"),
        P(("groups", "ctx", "sub"), "fsdp"),
        P("fsdp"),
        P("groups"),
        P("groups"),
    )
    return jax.shard_map(
        local,
        mesh=mesh,
        in_specs=placed,
        out_specs=(
            P(None, ("groups", "ctx", "sub"), "fsdp"),
            P("groups", None, "fsdp"),
            P(("groups", "ctx"), "fsdp"),
        ),
        check_vma=False,
    )
```

profile of v0, /device:TPU:0, one launch (start us, length us, event | category | flops | bytes accessed | tf_op | source)
XLA Modules:
  0.0 389.1 jit_solution(13309928368215574927)
XLA Ops:
  8.1 2.4 collective-permute-start
  10.5 1.8 fusion.231
  15.8 17.6 %all_gather.3 = bf16[128,2048]{1,0:T(8,128)(2,1)S(1)} all-gather(bf16[32,2048]{1,0:T(8,128)(2,1)} %param.15), channel_id=1, replica_groups=mesh['groups'=2,'ctx'=4,'fsdp'=2,'sub'=2] {'ctx'}, dimensions={0}, use_global_device_ids=true | all-gather | bytes 655360 | tf_op jit(solution)/shard_map/all_gather | solution.py:108
  33.5 9.7 %fusion.68 = (bf16[128,2048]{1,0:T(8,128)(2,1)S(1)}, bf16[128,2048]{1,0:T(8,128)(2,1)}, bf16[128,2048]{1,0:T(8,128)(2,1)}, bf16[128,2048]{1,0:T(8,128)(2,1)}) fusion(f32[2048]{0:T(1024)S(1)} %bitcast.486, pred[128]{0:T(512)(128)(4,1)S(1)} %get-tuple-element.922, f32[2048]{0:T(1024)S(1)} %bitcast.488, pred[128]{0:T(512)(128)(4,1)S(1)} %get-tuple-element.921, ...), kind=kLoop, calls=%fused_computation.240 | loop fusion | flops 28311552 | bytes 4907904 | tf_op jit(solution)/shard_map/convert_element_type | solution.py:107
  44.2 2.3 collective-permute-start.1
  47.9 1.8 fusion.77
  50.9 68.4 %while.35 = (s32[]{:T(128)}, f32[128,2048]{1,0:T(8,128)}, s32[128]{0:T(128)S(1)}, f32[128,2048]{1,0:T(8,128)}, bf16[255,2048]{1,0:T(8,128)(2,1)S(1)}, /*index=5*...) while((s32[]{:T(128)}, f32[128,2048]{1,0:T(8,128)}, ...), condition=%wide.region_4.5_spmd.clone, body=%wide.region_3.4_spmd.clone.sunk | while | flops 17041540 | bytes 10885599 | solution.py:46
  51.1 1.7 constant_dynamic-slice_fusion.35
  52.9 5.7 %fusion.242 = f32[128,2048]{1,0:T(8,128)} fusion(f32[128,2048]{1,0:T(8,128)} %get-tuple-element.1254, bf16[255,2048]{1,0:T(8,128)(2,1)S(1)} %get-tuple-element.1297, s32[]{:T(128)S(6)} %select_n.2579, f32[2048]{0:T(1024)S(1)} %bitcast.441, s32[]{:T(128)S(6)} %select_n.2596, f32[2048]{0:T(1024)S(1)} %bitcast.442, s32[]{:T(128)S(6)} %select_n.2597, ...), kind=kLoop, calls=%fused_computation.80.clone.1 | loop fusion | flops 17039360 | bytes 10618945 | tf_op jit(solution)/shard_map/while/body/eval_jaxpr/add | solution.py:40
  58.6 1.8 constant_dynamic-slice_fusion.35
  60.7 6.7 %fusion.242 = f32[128,2048]{1,0:T(8,128)} fusion(f32[128,2048]{1,0:T(8,128)} %get-tuple-element.1254, bf16[255,2048]{1,0:T(8,128)(2,1)S(1)} %get-tuple-element.1297, s32[]{:T(128)S(6)} %select_n.2579, f32[2048]{0:T(1024)S(1)} %bitcast.441, s32[]{:T(128)S(6)} %select_n.2596, f32[2048]{0:T(1024)S(1)} %bitcast.442, s32[]{:T(128)S(6)} %select_n.2597, ...), kind=kLoop, calls=%fused_computation.80.clone.1 | loop fusion | flops 17039360 | bytes 10618945 | tf_op jit(solution)/shard_map/while/body/eval_jaxpr/add | solution.py:40
  69.2 6.7 %fusion.242 = f32[128,2048]{1,0:T(8,128)} fusion(f32[128,2048]{1,0:T(8,128)} %get-tuple-element.1254, bf16[255,2048]{1,0:T(8,128)(2,1)S(1)} %get-tuple-element.1297, s32[]{:T(128)S(6)} %select_n.2579, f32[2048]{0:T(1024)S(1)} %bitcast.441, s32[]{:T(128)S(6)} %select_n.2596, f32[2048]{0:T(1024)S(1)} %bitcast.442, s32[]{:T(128)S(6)} %select_n.2597, ...), kind=kLoop, calls=%fused_computation.80.clone.1 | loop fusion | flops 17039360 | bytes 10618945 | tf_op jit(solution)/shard_map/while/body/eval_jaxpr/add | solution.py:40
  75.9 1.9 constant_dynamic-slice_fusion.35
  77.9 6.7 %fusion.242 = f32[128,2048]{1,0:T(8,128)} fusion(f32[128,2048]{1,0:T(8,128)} %get-tuple-element.1254, bf16[255,2048]{1,0:T(8,128)(2,1)S(1)} %get-tuple-element.1297, s32[]{:T(128)S(6)} %select_n.2579, f32[2048]{0:T(1024)S(1)} %bitcast.441, s32[]{:T(128)S(6)} %select_n.2596, f32[2048]{0:T(1024)S(1)} %bitcast.442, s32[]{:T(128)S(6)} %select_n.2597, ...), kind=kLoop, calls=%fused_computation.80.clone.1 | loop fusion | flops 17039360 | bytes 10618945 | tf_op jit(solution)/shard_map/while/body/eval_jaxpr/add | solution.py:40
  84.7 1.6 constant_dynamic-slice_fusion.35
  86.5 6.7 %fusion.242 = f32[128,2048]{1,0:T(8,128)} fusion(f32[128,2048]{1,0:T(8,128)} %get-tuple-element.1254, bf16[255,2048]{1,0:T(8,128)(2,1)S(1)} %get-tuple-element.1297, s32[]{:T(128)S(6)} %select_n.2579, f32[2048]{0:T(1024)S(1)} %bitcast.441, s32[]{:T(128)S(6)} %select_n.2596, f32[2048]{0:T(1024)S(1)} %bitcast.442, s32[]{:T(128)S(6)} %select_n.2597, ...), kind=kLoop, calls=%fused_computation.80.clone.1 | loop fusion | flops 17039360 | bytes 10618945 | tf_op jit(solution)/shard_map/while/body/eval_jaxpr/add | solution.py:40
  93.2 1.9 constant_dynamic-slice_fusion.35
  95.3 6.7 %fusion.242 = f32[128,2048]{1,0:T(8,128)} fusion(f32[128,2048]{1,0:T(8,128)} %get-tuple-element.1254, bf16[255,2048]{1,0:T(8,128)(2,1)S(1)} %get-tuple-element.1297, s32[]{:T(128)S(6)} %select_n.2579, f32[2048]{0:T(1024)S(1)} %bitcast.441, s32[]{:T(128)S(6)} %select_n.2596, f32[2048]{0:T(1024)S(1)} %bitcast.442, s32[]{:T(128)S(6)} %select_n.2597, ...), kind=kLoop, calls=%fused_computation.80.clone.1 | loop fusion | flops 17039360 | bytes 10618945 | tf_op jit(solution)/shard_map/while/body/eval_jaxpr/add | solution.py:40
  103.8 6.7 %fusion.242 = f32[128,2048]{1,0:T(8,128)} fusion(f32[128,2048]{1,0:T(8,128)} %get-tuple-element.1254, bf16[255,2048]{1,0:T(8,128)(2,1)S(1)} %get-tuple-element.1297, s32[]{:T(128)S(6)} %select_n.2579, f32[2048]{0:T(1024)S(1)} %bitcast.441, s32[]{:T(128)S(6)} %select_n.2596, f32[2048]{0:T(1024)S(1)} %bitcast.442, s32[]{:T(128)S(6)} %select_n.2597, ...), kind=kLoop, calls=%fused_computation.80.clone.1 | loop fusion | flops 17039360 | bytes 10618945 | tf_op jit(solution)/shard_map/while/body/eval_jaxpr/add | solution.py:40
  110.5 1.9 constant_dynamic-slice_fusion.35
  112.6 6.7 %fusion.242 = f32[128,2048]{1,0:T(8,128)} fusion(f32[128,2048]{1,0:T(8,128)} %get-tuple-element.1254, bf16[255,2048]{1,0:T(8,128)(2,1)S(1)} %get-tuple-element.1297, s32[]{:T(128)S(6)} %select_n.2579, f32[2048]{0:T(1024)S(1)} %bitcast.441, s32[]{:T(128)S(6)} %select_n.2596, f32[2048]{0:T(1024)S(1)} %bitcast.442, s32[]{:T(128)S(6)} %select_n.2597, ...), kind=kLoop, calls=%fused_computation.80.clone.1 | loop fusion | flops 17039360 | bytes 10618945 | tf_op jit(solution)/shard_map/while/body/eval_jaxpr/add | solution.py:40
  119.3 2.1 convolution_bitcast_fusion
  121.7 33.0 %psum.21 = f32[8]{0:T(128)S(1)} all-reduce(f32[8]{0:T(128)S(1)} %convolution_bitcast_fusion.2), channel_id=1, replica_groups=mesh['groups'=2,'ctx'=4,'fsdp'=2,'sub'=2] {'ctx','fsdp','sub'}, use_global_device_ids=true, to_apply=%region_5.6 | all-reduce | flops 8 | bytes 64 | tf_op jit(solution)/shard_map/psum | solution.py:118
  155.0 2.2 fusion.66
  159.8 70.9 %while.34 = (s32[]{:T(128)}, f32[128,2048]{1,0:T(8,128)}, s32[128]{0:T(128)S(1)}, bf16[128,2048]{1,0:T(8,128)(2,1)}, bf16[255,2048]{1,0:T(8,128)(2,1)S(1)}, /*in...) while((s32[]{:T(128)}, f32[128,2048]{1,0:T(8,128)}, ...), condition=%wide.region_48.49_spmd, body=%wide.region_31.48_spmd.sunk | while | flops 17270864 | bytes 10098467 | solution.py:81
  159.9 3.8 fusion.241
  163.7 4.0 %fusion.240 = (f32[2048]{0:T(1024)S(1)}, f32[2048]{0:T(1024)S(1)}, f32[2048]{0:T(1024)S(1)}, f32[2048]{0:T(1024)S(1)}, f32[2048]{0:T(1024)S(1)}, /*index=5*/f32[...) fusion(bf16[128,2048]{1,0:T(8,128)(2,1)} %get-tuple-element.1548, bf16[255,2048]{1,0:T(8,128)(2,1)S(1)} %get-tuple-element.1549, ...), kind=kLoop, calls=%fused_computation.45.clone.1 | loop fusion | flops 8634368 | bytes 4785184 | tf_op jit(solution)/shard_map/while/body/eval_jaxpr/reduce_sum | solution.py:77
  168.8 3.8 fusion.241
  172.6 4.0 %fusion.240 = (f32[2048]{0:T(1024)S(1)}, f32[2048]{0:T(1024)S(1)}, f32[2048]{0:T(1024)S(1)}, f32[2048]{0:T(1024)S(1)}, f32[2048]{0:T(1024)S(1)}, /*index=5*/f32[...) fusion(bf16[128,2048]{1,0:T(8,128)(2,1)} %get-tuple-element.1548, bf16[255,2048]{1,0:T(8,128)(2,1)S(1)} %get-tuple-element.1549, ...), kind=kLoop, calls=%fused_computation.45.clone.1 | loop fusion | flops 8634368 | bytes 4785184 | tf_op jit(solution)/shard_map/while/body/eval_jaxpr/reduce_sum | solution.py:77
  177.6 3.8 fusion.241
  181.5 4.0 %fusion.240 = (f32[2048]{0:T(1024)S(1)}, f32[2048]{0:T(1024)S(1)}, f32[2048]{0:T(1024)S(1)}, f32[2048]{0:T(1024)S(1)}, f32[2048]{0:T(1024)S(1)}, /*index=5*/f32[...) fusion(bf16[128,2048]{1,0:T(8,128)(2,1)} %get-tuple-element.1548, bf16[255,2048]{1,0:T(8,128)(2,1)S(1)} %get-tuple-element.1549, ...), kind=kLoop, calls=%fused_computation.45.clone.1 | loop fusion | flops 8634368 | bytes 4785184 | tf_op jit(solution)/shard_map/while/body/eval_jaxpr/reduce_sum | solution.py:77
  186.5 3.8 fusion.241
  190.3 4.0 %fusion.240 = (f32[2048]{0:T(1024)S(1)}, f32[2048]{0:T(1024)S(1)}, f32[2048]{0:T(1024)S(1)}, f32[2048]{0:T(1024)S(1)}, f32[2048]{0:T(1024)S(1)}, /*index=5*/f32[...) fusion(bf16[128,2048]{1,0:T(8,128)(2,1)} %get-tuple-element.1548, bf16[255,2048]{1,0:T(8,128)(2,1)S(1)} %get-tuple-element.1549, ...), kind=kLoop, calls=%fused_computation.45.clone.1 | loop fusion | flops 8634368 | bytes 4785184 | tf_op jit(solution)/shard_map/while/body/eval_jaxpr/reduce_sum | solution.py:77
  195.4 3.8 fusion.241
  199.2 4.0 %fusion.240 = (f32[2048]{0:T(1024)S(1)}, f32[2048]{0:T(1024)S(1)}, f32[2048]{0:T(1024)S(1)}, f32[2048]{0:T(1024)S(1)}, f32[2048]{0:T(1024)S(1)}, /*index=5*/f32[...) fusion(bf16[128,2048]{1,0:T(8,128)(2,1)} %get-tuple-element.1548, bf16[255,2048]{1,0:T(8,128)(2,1)S(1)} %get-tuple-element.1549, ...), kind=kLoop, calls=%fused_computation.45.clone.1 | loop fusion | flops 8634368 | bytes 4785184 | tf_op jit(solution)/shard_map/while/body/eval_jaxpr/reduce_sum | solution.py:77
  204.2 3.8 fusion.241
  208.0 4.0 %fusion.240 = (f32[2048]{0:T(1024)S(1)}, f32[2048]{0:T(1024)S(1)}, f32[2048]{0:T(1024)S(1)}, f32[2048]{0:T(1024)S(1)}, f32[2048]{0:T(1024)S(1)}, /*index=5*/f32[...) fusion(bf16[128,2048]{1,0:T(8,128)(2,1)} %get-tuple-element.1548, bf16[255,2048]{1,0:T(8,128)(2,1)S(1)} %get-tuple-element.1549, ...), kind=kLoop, calls=%fused_computation.45.clone.1 | loop fusion | flops 8634368 | bytes 4785184 | tf_op jit(solution)/shard_map/while/body/eval_jaxpr/reduce_sum | solution.py:77
  213.1 3.8 fusion.241
  216.9 4.0 %fusion.240 = (f32[2048]{0:T(1024)S(1)}, f32[2048]{0:T(1024)S(1)}, f32[2048]{0:T(1024)S(1)}, f32[2048]{0:T(1024)S(1)}, f32[2048]{0:T(1024)S(1)}, /*index=5*/f32[...) fusion(bf16[128,2048]{1,0:T(8,128)(2,1)} %get-tuple-element.1548, bf16[255,2048]{1,0:T(8,128)(2,1)S(1)} %get-tuple-element.1549, ...), kind=kLoop, calls=%fused_computation.45.clone.1 | loop fusion | flops 8634368 | bytes 4785184 | tf_op jit(solution)/shard_map/while/body/eval_jaxpr/reduce_sum | solution.py:77
  221.9 3.8 fusion.241
  225.8 4.0 %fusion.240 = (f32[2048]{0:T(1024)S(1)}, f32[2048]{0:T(1024)S(1)}, f32[2048]{0:T(1024)S(1)}, f32[2048]{0:T(1024)S(1)}, f32[2048]{0:T(1024)S(1)}, /*index=5*/f32[...) fusion(bf16[128,2048]{1,0:T(8,128)(2,1)} %get-tuple-element.1548, bf16[255,2048]{1,0:T(8,128)(2,1)S(1)} %get-tuple-element.1549, ...), kind=kLoop, calls=%fused_computation.45.clone.1 | loop fusion | flops 8634368 | bytes 4785184 | tf_op jit(solution)/shard_map/while/body/eval_jaxpr/reduce_sum | solution.py:77
  230.7 3.3 fusion.134
  235.4 69.9 %while.36 = (s32[]{:T(128)}, f32[128,2048]{1,0:T(8,128)}, s32[255]{0:T(256)S(1)}, f32[128,2048]{1,0:T(8,128)}, bf16[255,2048]{1,0:T(8,128)(2,1)S(1)}, /*index=5*...) while((s32[]{:T(128)}, f32[128,2048]{1,0:T(8,128)}, ...), condition=%wide.region_8.9_spmd.clone, body=%wide.region_7.8_spmd.clone.sunk | while | flops 17041508 | bytes 10893119 | solution.py:65
  235.5 1.7 constant_dynamic-slice_fusion.36
  237.5 5.8 %fusion.243 = f32[128,2048]{1,0:T(8,128)} fusion(f32[128,2048]{1,0:T(8,128)} %get-tuple-element.1388, bf16[255,2048]{1,0:T(8,128)(2,1)S(1)} %get-tuple-element.1445, s32[]{:T(128)S(6)} %select_n.2627, f32[2048]{0:T(1024)S(1)} %bitcast.457, s32[]{:T(128)S(6)} %select_n.2644, f32[2048]{0:T(1024)S(1)} %bitcast.458, s32[]{:T(128)S(6)} %select_n.2645, ...), kind=kLoop, calls=%fused_computation.128.clone.1 | loop fusion | flops 17039360 | bytes 10618945 | tf_op jit(solution)/shard_map/while/body/eval_jaxpr/add | solution.py:59
  243.2 1.8 constant_dynamic-slice_fusion.36
  245.4 6.8 %fusion.243 = f32[128,2048]{1,0:T(8,128)} fusion(f32[128,2048]{1,0:T(8,128)} %get-tuple-element.1388, bf16[255,2048]{1,0:T(8,128)(2,1)S(1)} %get-tuple-element.1445, s32[]{:T(128)S(6)} %select_n.2627, f32[2048]{0:T(1024)S(1)} %bitcast.457, s32[]{:T(128)S(6)} %select_n.2644, f32[2048]{0:T(1024)S(1)} %bitcast.458, s32[]{:T(128)S(6)} %select_n.2645, ...), kind=kLoop, calls=%fused_computation.128.clone.1 | loop fusion | flops 17039360 | bytes 10618945 | tf_op jit(solution)/shard_map/while/body/eval_jaxpr/add | solution.py:59
  254.1 6.8 %fusion.243 = f32[128,2048]{1,0:T(8,128)} fusion(f32[128,2048]{1,0:T(8,128)} %get-tuple-element.1388, bf16[255,2048]{1,0:T(8,128)(2,1)S(1)} %get-tuple-element.1445, s32[]{:T(128)S(6)} %select_n.2627, f32[2048]{0:T(1024)S(1)} %bitcast.457, s32[]{:T(128)S(6)} %select_n.2644, f32[2048]{0:T(1024)S(1)} %bitcast.458, s32[]{:T(128)S(6)} %select_n.2645, ...), kind=kLoop, calls=%fused_computation.128.clone.1 | loop fusion | flops 17039360 | bytes 10618945 | tf_op jit(solution)/shard_map/while/body/eval_jaxpr/add | solution.py:59
  260.9 1.9 constant_dynamic-slice_fusion.36
  263.1 6.8 %fusion.243 = f32[128,2048]{1,0:T(8,128)} fusion(f32[128,2048]{1,0:T(8,128)} %get-tuple-element.1388, bf16[255,2048]{1,0:T(8,128)(2,1)S(1)} %get-tuple-element.1445, s32[]{:T(128)S(6)} %select_n.2627, f32[2048]{0:T(1024)S(1)} %bitcast.457, s32[]{:T(128)S(6)} %select_n.2644, f32[2048]{0:T(1024)S(1)} %bitcast.458, s32[]{:T(128)S(6)} %select_n.2645, ...), kind=kLoop, calls=%fused_computation.128.clone.1 | loop fusion | flops 17039360 | bytes 10618945 | tf_op jit(solution)/shard_map/while/body/eval_jaxpr/add | solution.py:59
  271.8 6.8 %fusion.243 = f32[128,2048]{1,0:T(8,128)} fusion(f32[128,2048]{1,0:T(8,128)} %get-tuple-element.1388, bf16[255,2048]{1,0:T(8,128)(2,1)S(1)} %get-tuple-element.1445, s32[]{:T(128)S(6)} %select_n.2627, f32[2048]{0:T(1024)S(1)} %bitcast.457, s32[]{:T(128)S(6)} %select_n.2644, f32[2048]{0:T(1024)S(1)} %bitcast.458, s32[]{:T(128)S(6)} %select_n.2645, ...), kind=kLoop, calls=%fused_computation.128.clone.1 | loop fusion | flops 17039360 | bytes 10618945 | tf_op jit(solution)/shard_map/while/body/eval_jaxpr/add | solution.py:59
  278.6 1.9 constant_dynamic-slice_fusion.36
  280.8 6.8 %fusion.243 = f32[128,2048]{1,0:T(8,128)} fusion(f32[128,2048]{1,0:T(8,128)} %get-tuple-element.1388, bf16[255,2048]{1,0:T(8,128)(2,1)S(1)} %get-tuple-element.1445, s32[]{:T(128)S(6)} %select_n.2627, f32[2048]{0:T(1024)S(1)} %bitcast.457, s32[]{:T(128)S(6)} %select_n.2644, f32[2048]{0:T(1024)S(1)} %bitcast.458, s32[]{:T(128)S(6)} %select_n.2645, ...), kind=kLoop, calls=%fused_computation.128.clone.1 | loop fusion | flops 17039360 | bytes 10618945 | tf_op jit(solution)/shard_map/while/body/eval_jaxpr/add | solution.py:59
  289.5 6.8 %fusion.243 = f32[128,2048]{1,0:T(8,128)} fusion(f32[128,2048]{1,0:T(8,128)} %get-tuple-element.1388, bf16[255,2048]{1,0:T(8,128)(2,1)S(1)} %get-tuple-element.1445, s32[]{:T(128)S(6)} %select_n.2627, f32[2048]{0:T(1024)S(1)} %bitcast.457, s32[]{:T(128)S(6)} %select_n.2644, f32[2048]{0:T(1024)S(1)} %bitcast.458, s32[]{:T(128)S(6)} %select_n.2645, ...), kind=kLoop, calls=%fused_computation.128.clone.1 | loop fusion | flops 17039360 | bytes 10618945 | tf_op jit(solution)/shard_map/while/body/eval_jaxpr/add | solution.py:59
  296.2 1.9 constant_dynamic-slice_fusion.36
  298.5 6.8 %fusion.243 = f32[128,2048]{1,0:T(8,128)} fusion(f32[128,2048]{1,0:T(8,128)} %get-tuple-element.1388, bf16[255,2048]{1,0:T(8,128)(2,1)S(1)} %get-tuple-element.1445, s32[]{:T(128)S(6)} %select_n.2627, f32[2048]{0:T(1024)S(1)} %bitcast.457, s32[]{:T(128)S(6)} %select_n.2644, f32[2048]{0:T(1024)S(1)} %bitcast.458, s32[]{:T(128)S(6)} %select_n.2645, ...), kind=kLoop, calls=%fused_computation.128.clone.1 | loop fusion | flops 17039360 | bytes 10618945 | tf_op jit(solution)/shard_map/while/body/eval_jaxpr/add | solution.py:59
  305.3 3.1 fusion.155
  311.8 2.0 fusion.157
  314.7 2.7 fusion.178
  319.8 1.7 fusion.120
  321.6 1.7 fusion.143
  323.4 1.7 fusion.166
  326.4 52.6 %all-reduce.3.cloned.1.call-done = (f32[3,7,2048]{2,1,0:T(8,128)}, f32[128,2048]{1,0:T(8,128)}) async-done(((f32[3,7,2048]{2,1,0:T(8,128)}, f32[128,2048]{1,0:T(8,128)}), (f32[3,7,2048]{2,1,0:T(8,128)}, f32[128,2048]{1,0:T(8,128)})) %all-reduce.3.cloned.1.call-update) | async-done | bytes 1220624 | tf_op jit(solution)/shard_map/psum | solution.py:140
  379.0 1.7 constant_dynamic-slice_fusion.32
  (231 shorter events, 38.8 us)
Async XLA Ops:
  7.2 371.8 %all-reduce.3.cloned.1.call-start = ((), (), s32[]{:S(2)}) async-start(), calls=%async_computation | async-start | bytes 2490368 | tf_op jit(solution)/shard_map/psum | solution.py:140
  8.1 25.3 %collective-permute-start = (bf16[3,6,2048]{2,1,0:T(8,128)(2,1)S(1)}, bf16[3,6,2048]{2,1,0:T(8,128)(2,1)S(1)}, u32[]{:S(2)}, u32[]{:S(2)}) collective-permute-start(bf16[3,6,2048]{2,1,0:T(8,128)(2,1)S(1)} %slice.171), channel_id=1, source_target_pairs={{0,1},{1,4},{4,5},{5,8},{8,9},{9,12},{12,13},{2,3},{3,6},{6,7},{7,... | collective-permute-start | bytes 221192 | tf_op jit(solution)/shard_map/ppermute | solution.py:16
  12.4 30.8 %copy-start.10 = (f32[1,1,2048]{2,1,0:T(1,128)}, f32[1,1,2048]{2,1,0:T(1,128)S(1)}, u32[]{:S(2)}) copy-start(f32[1,1,2048]{2,1,0:T(1,128)S(1)} %get-tuple-element.899) | copy-start | bytes 24580
  12.4 30.8 %copy-start.12 = (f32[1,1,2048]{2,1,0:T(1,128)}, f32[1,1,2048]{2,1,0:T(1,128)S(1)}, u32[]{:S(2)}) copy-start(f32[1,1,2048]{2,1,0:T(1,128)S(1)} %get-tuple-element.900) | copy-start | bytes 24580
  12.4 30.8 %copy-start.14 = (f32[1,1,2048]{2,1,0:T(1,128)}, f32[1,1,2048]{2,1,0:T(1,128)S(1)}, u32[]{:S(2)}) copy-start(f32[1,1,2048]{2,1,0:T(1,128)S(1)} %get-tuple-element.901) | copy-start | bytes 24580
  12.4 30.8 %copy-start.16 = (f32[1,1,2048]{2,1,0:T(1,128)}, f32[1,1,2048]{2,1,0:T(1,128)S(1)}, u32[]{:S(2)}) copy-start(f32[1,1,2048]{2,1,0:T(1,128)S(1)} %get-tuple-element.902) | copy-start | bytes 24580
  12.4 30.8 %copy-start.18 = (f32[1,1,2048]{2,1,0:T(1,128)}, f32[1,1,2048]{2,1,0:T(1,128)S(1)}, u32[]{:S(2)}) copy-start(f32[1,1,2048]{2,1,0:T(1,128)S(1)} %get-tuple-element.903) | copy-start | bytes 24580
  12.4 30.8 %copy-start.20 = (f32[1,1,2048]{2,1,0:T(1,128)}, f32[1,1,2048]{2,1,0:T(1,128)S(1)}, u32[]{:S(2)}) copy-start(f32[1,1,2048]{2,1,0:T(1,128)S(1)} %get-tuple-element.904) | copy-start | bytes 24580
  12.4 30.8 %copy-start.22 = (f32[1,1,2048]{2,1,0:T(1,128)}, f32[1,1,2048]{2,1,0:T(1,128)S(1)}, u32[]{:S(2)}) copy-start(f32[1,1,2048]{2,1,0:T(1,128)S(1)} %get-tuple-element.905) | copy-start | bytes 24580
  12.4 30.8 %copy-start.24 = (f32[1,1,2048]{2,1,0:T(1,128)}, f32[1,1,2048]{2,1,0:T(1,128)S(1)}, u32[]{:S(2)}) copy-start(f32[1,1,2048]{2,1,0:T(1,128)S(1)} %get-tuple-element.906) | copy-start | bytes 24580
  12.4 35.3 %copy-start.26 = (f32[1,1,2048]{2,1,0:T(1,128)}, f32[1,1,2048]{2,1,0:T(1,128)S(1)}, u32[]{:S(2)}) copy-start(f32[1,1,2048]{2,1,0:T(1,128)S(1)} %get-tuple-element.894) | copy-start | bytes 24580
  12.4 35.3 %copy-start.28 = (f32[1,1,2048]{2,1,0:T(1,128)}, f32[1,1,2048]{2,1,0:T(1,128)S(1)}, u32[]{:S(2)}) copy-start(f32[1,1,2048]{2,1,0:T(1,128)S(1)} %get-tuple-element.907) | copy-start | bytes 24580
  12.5 35.3 %copy-start.30 = (f32[1,1,2048]{2,1,0:T(1,128)}, f32[1,1,2048]{2,1,0:T(1,128)S(1)}, u32[]{:S(2)}) copy-start(f32[1,1,2048]{2,1,0:T(1,128)S(1)} %get-tuple-element.908) | copy-start | bytes 24580
  12.5 35.3 %copy-start.32 = (f32[1,1,2048]{2,1,0:T(1,128)}, f32[1,1,2048]{2,1,0:T(1,128)S(1)}, u32[]{:S(2)}) copy-start(f32[1,1,2048]{2,1,0:T(1,128)S(1)} %get-tuple-element.909) | copy-start | bytes 24580
  12.5 35.3 %copy-start.34 = (f32[1,1,2048]{2,1,0:T(1,128)}, f32[1,1,2048]{2,1,0:T(1,128)S(1)}, u32[]{:S(2)}) copy-start(f32[1,1,2048]{2,1,0:T(1,128)S(1)} %get-tuple-element.910) | copy-start | bytes 24580
  12.5 35.3 %copy-start.36 = (f32[1,1,2048]{2,1,0:T(1,128)}, f32[1,1,2048]{2,1,0:T(1,128)S(1)}, u32[]{:S(2)}) copy-start(f32[1,1,2048]{2,1,0:T(1,128)S(1)} %get-tuple-element.911) | copy-start | bytes 24580
  12.5 35.3 %copy-start.38 = (f32[1,1,2048]{2,1,0:T(1,128)}, f32[1,1,2048]{2,1,0:T(1,128)S(1)}, u32[]{:S(2)}) copy-start(f32[1,1,2048]{2,1,0:T(1,128)S(1)} %get-tuple-element.912) | copy-start | bytes 24580
  13.4 29.8 %copy-start.40 = (f32[1,1,2048]{2,1,0:T(1,128)}, f32[1,1,2048]{2,1,0:T(1,128)S(1)}, u32[]{:S(2)}) copy-start(f32[1,1,2048]{2,1,0:T(1,128)S(1)} %get-tuple-element.913) | copy-start | bytes 24580
  13.5 29.8 %copy-start.42 = (f32[1,1,2048]{2,1,0:T(1,128)}, f32[1,1,2048]{2,1,0:T(1,128)S(1)}, u32[]{:S(2)}) copy-start(f32[1,1,2048]{2,1,0:T(1,128)S(1)} %get-tuple-element.914) | copy-start | bytes 24580
  15.1 31.6 %copy-start.7 = (s32[255]{0:T(256)}, s32[255]{0:T(256)S(1)}, u32[]{:S(2)}) copy-start(s32[255]{0:T(256)S(1)} %fusion.225) | copy-start | bytes 3064
  15.8 32.1 %copy-start.47 = (pred[128]{0:T(512)(128)(4,1)}, pred[128]{0:T(512)(128)(4,1)S(1)}, u32[]{:S(2)}) copy-start(pred[128]{0:T(512)(128)(4,1)S(1)} %get-tuple-element.922) | copy-start | bytes 388
  15.8 32.1 %copy-start.49 = (pred[128]{0:T(512)(128)(4,1)}, pred[128]{0:T(512)(128)(4,1)S(1)}, u32[]{:S(2)}) copy-start(pred[128]{0:T(512)(128)(4,1)S(1)} %get-tuple-element.917) | copy-start | bytes 388
  15.8 32.1 %copy-start.51 = (pred[128]{0:T(512)(128)(4,1)}, pred[128]{0:T(512)(128)(4,1)S(1)}, u32[]{:S(2)}) copy-start(pred[128]{0:T(512)(128)(4,1)S(1)} %get-tuple-element.918) | copy-start | bytes 388
  15.8 32.1 %copy-start.53 = (pred[128]{0:T(512)(128)(4,1)}, pred[128]{0:T(512)(128)(4,1)S(1)}, u32[]{:S(2)}) copy-start(pred[128]{0:T(512)(128)(4,1)S(1)} %get-tuple-element.919) | copy-start | bytes 388
  15.8 32.1 %copy-start.55 = (pred[128]{0:T(512)(128)(4,1)}, pred[128]{0:T(512)(128)(4,1)S(1)}, u32[]{:S(2)}) copy-start(pred[128]{0:T(512)(128)(4,1)S(1)} %get-tuple-element.920) | copy-start | bytes 388
  15.8 32.1 %copy-start.57 = (pred[128]{0:T(512)(128)(4,1)}, pred[128]{0:T(512)(128)(4,1)S(1)}, u32[]{:S(2)}) copy-start(pred[128]{0:T(512)(128)(4,1)S(1)} %get-tuple-element.921) | copy-start | bytes 388
  33.5 13.0 %copy-start.67 = (s32[8]{0:T(128)S(1)}, s32[8]{0:T(128)}, u32[]{:S(2)}) copy-start(s32[8]{0:T(128)} %param.19) | copy-start | bytes 100
  43.3 0.8 copy-start.2
  43.3 4.6 %copy-start = (bf16[3,128,2048]{2,1,0:T(8,128)(2,1)S(1)}, bf16[3,128,2048]{2,1,0:T(8,128)(2,1)}, u32[]{:S(2)}) copy-start(bf16[3,128,2048]{2,1,0:T(8,128)(2,1)} %param.13) | copy-start | bytes 4718596
  44.2 5.5 %collective-permute-start.1 = (bf16[127,2048]{1,0:T(8,128)(2,1)S(1)}, bf16[127,2048]{1,0:T(8,128)(2,1)}, u32[]{:S(2)}, u32[]{:S(2)}) collective-permute-start(bf16[127,2048]{1,0:T(8,128)(2,1)S(1)} %slice.175), channel_id=1, source_target_pairs={{0,1},{1,4},{4,5},{5,8},{8,9},{9,12},{12,13},{2,3},{3,6},{6,7},{7,... | collective-permute-start | bytes 1560584 | tf_op jit(solution)/shard_map/ppermute | solution.py:16
  47.8 1.9 copy-start.3
  49.7 1.2 slice-start
  50.9 68.4 %copy-start.9 = (f32[2048]{0:T(1024)S(1)}, f32[2048]{0:T(1024)}, u32[]{:S(2)}) copy-start(f32[2048]{0:T(1024)} %param.17) | copy-start | bytes 24580
  50.9 103.7 %copy-start.66 = (s32[8]{0:T(128)S(1)}, s32[8]{0:T(128)}, u32[]{:S(2)}) copy-start(s32[8]{0:T(128)} %param.18) | copy-start | bytes 100
  50.9 103.7 %copy-start.68 = (s32[8]{0:T(128)S(1)}, s32[8]{0:T(128)}, u32[]{:S(2)}) copy-start(s32[8]{0:T(128)} %param.19) | copy-start | bytes 100
  155.0 4.8 %copy-start.65 = (f32[128]{0:T(128)}, f32[128]{0:T(128)S(1)}, u32[]{:S(2)}) copy-start(f32[128]{0:T(128)S(1)} %convolution_bitcast_fusion.1) | copy-start | bytes 1540
  157.2 76.8 %collective-permute-start.2 = (bf16[127,2048]{1,0:T(8,128)(2,1)}, bf16[127,2048]{1,0:T(8,128)(2,1)}, u32[]{:S(2)}, u32[]{:S(2)}) collective-permute-start(bf16[127,2048]{1,0:T(8,128)(2,1)} %bitcast.321), channel_id=1, source_target_pairs={{1,0},{4,1},{5,4},{8,5},{9,8},{12,9},{13,12},{3,2},{6,3},{7,6},{10... | collective-permute-start | bytes 1560584 | tf_op jit(solution)/shard_map/ppermute | solution.py:16
  159.8 71.0 %copy-start.4 = (bf16[128,2048]{1,0:T(8,128)(2,1)S(1)}, bf16[128,2048]{1,0:T(8,128)(2,1)}, u32[]{:S(2)}) copy-start(bf16[128,2048]{1,0:T(8,128)(2,1)} %param.16) | copy-start | bytes 1572868
  234.0 1.3 copy-start.8
  235.3 69.9 %copy-start.56 = (pred[128]{0:T(512)(128)(4,1)S(1)}, pred[128]{0:T(512)(128)(4,1)}, u32[]{:S(2)}) copy-start(pred[128]{0:T(512)(128)(4,1)} %copy-done.55) | copy-start | bytes 388
  235.4 69.9 %copy-start.58 = (pred[128]{0:T(512)(128)(4,1)S(1)}, pred[128]{0:T(512)(128)(4,1)}, u32[]{:S(2)}) copy-start(pred[128]{0:T(512)(128)(4,1)} %copy-done.57) | copy-start | bytes 388
  305.2 3.2 copy-start.1
  305.2 3.2 copy-start.5
  305.2 3.2 copy-start.6
  305.3 3.1 copy-start.48
  309.5 2.2 copy-start.44
  309.5 2.3 copy-start.50
  309.5 2.3 copy-start.52
  309.5 2.3 copy-start.54
  310.2 8.9 %collective-permute-start.3 = (bf16[3,6,2048]{2,1,0:T(8,128)(2,1)}, bf16[3,6,2048]{2,1,0:T(8,128)(2,1)S(1)}, u32[]{:S(2)}, u32[]{:S(2)}) collective-permute-start(bf16[3,6,2048]{2,1,0:T(8,128)(2,1)} %pad_maximum_fusion.6), channel_id=1, source_target_pairs={{1,0},{4,1},{5,4},{8,5},{9,8},{12,9},{13,12},{3,2},{6,3},{7,6},{10... | collective-permute-start | bytes 221192 | tf_op jit(solution)/shard_map/ppermute | solution.py:16
  313.8 3.6 copy-start.45
  313.8 3.6 copy-start.46
  319.0 0.7 copy-start.37
  319.0 0.7 copy-start.39
  319.7 1.8 copy-start.13
  319.7 1.8 copy-start.15
  319.8 1.8 copy-start.17
  319.8 1.8 copy-start.19
  319.8 1.8 copy-start.21
  319.8 1.8 copy-start.23
  319.8 1.8 copy-start.25
  321.6 1.8 copy-start.11
  321.6 1.8 copy-start.41
  321.6 1.8 copy-start.43
  (11 other events, 7.8 us)
Sparse Core Ops, SparseCore 0:
  319.0 59.9 all-reduce.2
where the time goes:
time: 392 us; the launch traced here: 389 us
  other arithmetic  210 us (54%)
  waiting for transfers between devices  52.6 us (13%)
  blocking collectives  50.6 us (13%)
  local copies, waits for them, and re-layouts  46.6 us (12%)
  between operations  15 us (4%)
  starting transfers between devices  7.62 us (2%)
    reduce_sum x21, other arithmetic, correlate_advance(): jnp.sum(jnp.where((row_age >= j)[:, None], product, 0.0), axis=0)  74.8 us
    add x8, other arithmetic, reverse_advance(): running + jnp.where(keep[:, None], weight_row[None, :] * window.astype(jn...  53.1 us
    add x8, other arithmetic, causal_advance(): running + jnp.where((row_age >= j)[:, None], weight_row[None, :] * window...  52.7 us
    psum x1, waiting for transfers between devices, local(): filter_all, d_feat = lax.psum((filter_part, taps_part), ('ctx', 'sub'))  52.6 us
    psum x1, blocking collectives, local(): totals = lax.psum(partial_sums, ('ctx', 'fsdp', 'sub'))  33 us
    all_gather x1, blocking collectives, local(): lax.all_gather(long_filter, 'ctx', axis=0, tiled=True).astype(jnp.float32)  17.6 us
    dynamic_slice x9, local copies, waits for them, and re-layouts, reverse_advance(): weight_row = lax.dynamic_index_in_dim(tap_table, j, 0, keepdims=False)  15.9 us
    dynamic_slice x9, local copies, waits for them, and re-layouts, causal_advance(): weight_row = lax.dynamic_index_in_dim(tap_table, j, 0, keepdims=False)  15 us
  transfers between devices with their start and end apart: 5, of which 1 were waited for; matrix products, arithmetic and copies ran while one was open for 25% of the time, Pallas kernels for 0%

commit v1 on v0

v1 whole, which is shorter than its diff:
```python
import jax
import jax.numpy as jnp
import numpy as np
from jax import lax
from jax.experimental import pallas as pl
from jax.experimental.pallas import tpu as pltpu
from jax.sharding import PartitionSpec as P

LH = 128
KF = 7
RIM = 16
BF = jnp.bfloat16
F32 = jnp.float32
VMEM_LIMIT = 48 * 1024 * 1024


def passed_along(value, axis, steps):
    count = lax.axis_size(axis)
    leading, last = (max(0, -steps), min(count, count - steps))
    return lax.ppermute(value, axis, [(source, source + steps) for source in range(leading, last)])


def swapped(value, axis, distance):
    count = lax.axis_size(axis)
    return lax.ppermute(value, axis, [(source, source ^ distance) for source in range(count)])


def rotated(value, axis, distance):
    count = lax.axis_size(axis)
    return lax.ppermute(value, axis, [(source, (source + distance) % count) for source in range(count)])


def summed_everywhere(value):
    for axis in ("sub", "fsdp", "ctx"):
        distance = 1
        while distance < lax.axis_size(axis):
            value = value + swapped(value, axis, distance)
            distance *= 2
    return value


def half_wave(rows):
    odd = 2 * np.arange(rows)[:, None] + 1
    span = np.arange(-rows, 2 * rows)[None, :]
    angle = np.pi * ((odd * span) % (4 * rows)) / (2 * rows)
    table = np.concatenate([np.cos(angle), -np.sin(angle)], axis=0)
    before, own, after = np.split(table, 3, axis=1)
    back = own.T / rows
    as_f32 = lambda parts: np.concatenate(parts, axis=1).astype(np.float32)
    return as_f32([own, after]), as_f32([own, before]), as_f32([own]), as_f32([back])


def dot(left, right):
    return jnp.dot(left, right, preferred_element_type=F32)


class Layout:
    def __init__(self, len_ref, rows, tokens):
        self.rows, self.tokens = rows, tokens
        self.count = len_ref.shape[0]
        self.base = (lax.axis_index("ctx") * lax.axis_size("sub") + lax.axis_index("sub")) * rows
        offset = jnp.int32(0)
        self.offsets = []
        for s in range(self.count):
            self.offsets.append(offset)
            offset = offset + len_ref[s]

    def segment(self, position):
        seg = jnp.zeros_like(position)
        for s in range(1, self.count):
            seg = seg + jnp.where(position >= self.offsets[s], 1, 0)
        return jnp.where((position >= 0) & (position < self.tokens), seg, -1)

    def age(self, position):
        start = jnp.zeros_like(position)
        for s in range(1, self.count):
            start = jnp.where(position >= self.offsets[s], self.offsets[s], start)
        return position - start

    def scalar_segment(self, position):
        seg = jnp.int32(0)
        for s in range(1, self.count):
            seg = seg + jnp.where(position >= self.offsets[s], 1, 0)
        return seg

    def span(self):
        return self.scalar_segment(self.base), self.scalar_segment(self.base + self.rows - 1) + 1


def causal_shifts(sm_ref, layout, first):
    rows = layout.rows
    row = lax.broadcasted_iota(jnp.int32, (rows, rows + RIM), 0)
    col = lax.broadcasted_iota(jnp.int32, (rows, rows + RIM), 1)
    age = layout.age(layout.base + first + row)
    for j in range(KF):
        hit = (col == row + (RIM - j)) & (age >= j)
        sm_ref[j * rows : (j + 1) * rows, :] = jnp.where(hit, 1.0, 0.0).astype(BF)


def reverse_shifts(sm_ref, layout):
    rows = layout.rows
    row = lax.broadcasted_iota(jnp.int32, (rows, rows + RIM), 0)
    col = lax.broadcasted_iota(jnp.int32, (rows, rows + RIM), 1)
    age = layout.age(layout.base + col)
    for j in range(KF):
        hit = (col == row + j) & (age >= j)
        sm_ref[j * rows : (j + 1) * rows, :] = jnp.where(hit, 1.0, 0.0).astype(BF)


def tap_sum(sm_ref, taps, x, rows):
    total = None
    for j in range(KF):
        term = dot(sm_ref[j * rows : (j + 1) * rows, :], x) * taps[j : j + 1, :]
        total = term if total is None else total + term
    return total


def feat_kernel(tokens, len_ref, s_ref, halo_ref, taps_ref, q_ref, k_ref, v_ref, z_ref, sm_ref):
    rows = s_ref.shape[1]

    @pl.when(pl.program_id(0) == 0)
    def _():
        causal_shifts(sm_ref, Layout(len_ref, rows, tokens), 0)

    feats = []
    for i, out in enumerate((q_ref, k_ref, v_ref)):
        x = jnp.concatenate([halo_ref[i], s_ref[i]], axis=0)
        feat = tap_sum(sm_ref, taps_ref[i], x, rows).astype(BF)
        out[...] = feat
        feats.append(feat)
    z_ref[...] = (feats[1].astype(F32) * feats[2].astype(F32)).astype(BF)


def segment_columns(ref, layout, first_own, first_rim):
    rows = layout.rows
    col = lax.broadcasted_iota(jnp.int32, ref.shape, 1)
    position = layout.base + jnp.where(col < rows, col + first_own, col - rows + first_rim)
    ref[...] = layout.segment(position).astype(F32)


def segment_rows(ref, layout):
    row = lax.broadcasted_iota(jnp.int32, ref.shape, 0)
    ref[...] = layout.segment(layout.base + row).astype(F32)


def kept(table, seg_table, s):
    return jnp.where(seg_table == s.astype(F32), table, 0.0).astype(BF)


def times(a, b, rows):
    ar, ai, br, bi = a[:rows], a[rows:], b[:rows], b[rows:]
    return jnp.concatenate([ar * br - ai * bi, ar * bi + ai * br], axis=0)


def conj_times(a, b, rows):
    ar, ai, br, bi = a[:rows], a[rows:], b[:rows], b[rows:]
    return jnp.concatenate([ar * br + ai * bi, ar * bi - ai * br], axis=0)


def dzq_kernel(tokens, len_ref, tail_ref, sqn_ref, taps_ref, mine_ref, other_ref, q_ref, z_ref, dir_ref,
               ahead_ref, own_ref, back_ref,
               dzq_ref, qn_ref, h_ref, part_ref, sm_ref, segc_ref, segr_ref, filt_ref):
    rows = q_ref.shape[0]
    layout = Layout(len_ref, rows, tokens)
    step = pl.program_id(0)

    @pl.when(step == 0)
    def _():
        causal_shifts(sm_ref, layout, rows)
        segment_columns(segc_ref, layout, 0, rows)
        segment_rows(segr_ref, layout)
        part_ref[...] = jnp.zeros_like(part_ref)

    x = jnp.concatenate([tail_ref[0], sqn_ref[...]], axis=0)
    qn = tap_sum(sm_ref, taps_ref[0], x, rows).astype(BF)
    qn_ref[...] = qn
    shards, shard = mine_ref.shape[0], mine_ref.shape[1]
    half = jnp.where(step < pl.num_programs(0) // 2, 0, 1)
    here = half == lax.axis_index("sub")
    for d in range(shards):
        at = lax.rem(lax.axis_index("ctx") + (shards - d), shards) * shard
        filt_ref[pl.ds(pl.multiple_of(at, 8), shard), :] = jnp.where(here, mine_ref[d].astype(F32), other_ref[d].astype(F32))
    h = dot(own_ref[...].astype(BF), filt_ref[...].astype(BF))
    h_ref[...] = h
    q_ext = jnp.concatenate([q_ref[...], qn], axis=0)
    dzq_ref[...] = jnp.zeros_like(dzq_ref)
    first, end = layout.span()

    def one_segment(s, carry):
        spectrum = dot(kept(ahead_ref[...], segc_ref[...], s), q_ext)
        g = conj_times(h_ref[...], spectrum, rows).astype(BF)
        term = dot(kept(back_ref[...], segr_ref[...], s), g)
        dzq_ref[...] += term
        prod = term * z_ref[...].astype(F32) * dir_ref[...]
        row = jnp.sum(prod, axis=0, keepdims=True)
        lanes = row[:, :128]
        for c in range(128, row.shape[1], 128):
            lanes = lanes + row[:, c : c + 128]
        part_ref[pl.ds(s, 1), :] += lanes
        return carry

    lax.fori_loop(first, end, one_segment, 0)


def w_kernel(tokens, len_ref, z_ref, zp_ref, h_ref, behind_ref, back_ref, w_ref, segc_ref, segr_ref):
    rows = z_ref.shape[0]
    layout = Layout(len_ref, rows, tokens)

    @pl.when(pl.program_id(0) == 0)
    def _():
        segment_columns(segc_ref, layout, 0, -rows)
        segment_rows(segr_ref, layout)

    z_ext = jnp.concatenate([z_ref[...], zp_ref[...]], axis=0)
    w_ref[...] = jnp.zeros_like(w_ref)
    first, end = layout.span()

    def one_segment(s, carry):
        spectrum = dot(kept(behind_ref[...], segc_ref[...], s), z_ext)
        g = times(h_ref[...], spectrum, rows).astype(BF)
        w_ref[...] += dot(kept(back_ref[...], segr_ref[...], s), g)
        return carry

    lax.fori_loop(first, end, one_segment, 0)


def dzu_kernel(tokens, len_ref, q_ref, qn_ref, up_ref, upn_ref, h_ref, ahead_ref, back_ref, dzu_ref, segc_ref, segr_ref):
    rows = q_ref.shape[0]
    layout = Layout(len_ref, rows, tokens)

    @pl.when(pl.program_id(0) == 0)
    def _():
        segment_columns(segc_ref, layout, 0, rows)
        segment_rows(segr_ref, layout)

    own = (q_ref[...].astype(F32) * up_ref[...].astype(F32)).astype(BF)
    rim = (qn_ref[...].astype(F32) * upn_ref[...].astype(F32)).astype(BF)
    u_ext = jnp.concatenate([own, rim], axis=0)
    dzu_ref[...] = jnp.zeros_like(dzu_ref)
    first, end = layout.span()

    def one_segment(s, carry):
        spectrum = dot(kept(ahead_ref[...], segc_ref[...], s), u_ext)
        g = conj_times(h_ref[...], spectrum, rows).astype(BF)
        dzu_ref[...] += dot(kept(back_ref[...], segr_ref[...], s), g)
        return carry

    lax.fori_loop(first, end, one_segment, 0)


def coefficients(len_ref, ids_ref, part_ref):
    count = len_ref.shape[0]
    index = lax.broadcasted_iota(jnp.int32, (count, 128), 0)
    length = jnp.zeros((count, 128), F32)
    ids = jnp.zeros((count, 128), jnp.int32)
    for s in range(count):
        length = jnp.where(index == s, len_ref[s].astype(F32), length)
        ids = jnp.where(index == s, ids_ref[s], ids)
    scores = jnp.broadcast_to(jnp.sum(part_ref[...], axis=1, keepdims=True), (count, 128)) / length
    total = jnp.zeros((count, 128), F32)
    mates = jnp.zeros((count, 128), F32)
    for s in range(count):
        same = jnp.where(ids == ids_ref[s], 1.0, 0.0)
        mates = mates + same
        total = total + same * scores[s : s + 1, :]
    return (scores - total / mates) / length


def token_coefficients(coef, seg):
    spread = jnp.zeros(seg.shape, F32)
    for s in range(coef.shape[0]):
        spread = jnp.where(seg == s, coef[s : s + 1, :], spread)
    return spread


def across(column, width):
    return jnp.concatenate([column] * (width // 128), axis=1)


def dfilter_kernel(tokens, sub_ref, len_ref, ids_ref, part_ref, z_ref, q_ref, qn_ref, up_ref, upn_ref, dir_ref,
                   ahead_ref, own_ref, back_ref, send_ref, keep_ref, segc_ref, coef_ref, acc_ref):
    rows, width = z_ref.shape
    layout = Layout(len_ref, rows, tokens)
    step = pl.program_id(0)

    @pl.when(step == 0)
    def _():
        segment_columns(segc_ref, layout, 0, rows)
        coef = coefficients(len_ref, ids_ref, part_ref)
        position = layout.base + lax.broadcasted_iota(jnp.int32, (2 * rows, 128), 0)
        coef_ref[...] = token_coefficients(coef, layout.segment(position))

    parts = []
    for n, (q, up) in enumerate(((q_ref, up_ref), (qn_ref, upn_ref))):
        dy = up[...].astype(F32) + across(coef_ref[n * rows : (n + 1) * rows, :], width) * dir_ref[...]
        parts.append((dy * q[...].astype(F32)).astype(BF))
    dw_ext = jnp.concatenate(parts, axis=0)
    acc_ref[...] = jnp.zeros_like(acc_ref)
    first, end = layout.span()

    def one_segment(s, carry):
        z_spec = dot(kept(own_ref[...], segc_ref[:, :rows], s), z_ref[...])
        spectrum = dot(kept(ahead_ref[...], segc_ref[...], s), dw_ext)
        acc_ref[...] += conj_times(z_spec, spectrum, rows)
        return carry

    lax.fori_loop(first, end, one_segment, 0)
    result = dot(back_ref[...].astype(BF), acc_ref[...].astype(BF))
    half = pl.num_programs(0) // 2

    @pl.when(step < half)
    def _():
        send_ref[...] = result.astype(BF)

    @pl.when(step >= half)
    def _():
        keep_ref[...] = result


def grads_kernel(tokens, sub_ref, len_ref, ids_ref, part_ref, s_ref, halo_ref, q_ref, k_ref, v_ref, up_ref, dir_ref,
                 w_ref, dzu_ref, dzq_ref, da_ref, send_ref, keep_ref, sm_ref, coef_ref):
    rows, width = q_ref.shape
    layout = Layout(len_ref, rows, tokens)
    step = pl.program_id(0)

    @pl.when(step == 0)
    def _():
        causal_shifts(sm_ref, layout, 0)
        coef = coefficients(len_ref, ids_ref, part_ref)
        position = layout.base + lax.broadcasted_iota(jnp.int32, (rows, 128), 0)
        coef_ref[...] = token_coefficients(coef, layout.segment(position))

    rise = across(coef_ref[...], width) * dir_ref[...]
    dz = dzu_ref[...] + rise * dzq_ref[...]
    dq = ((up_ref[...].astype(F32) + rise) * w_ref[...]).astype(BF)
    dk = (dz * v_ref[...].astype(F32)).astype(BF)
    dv = (dz * k_ref[...].astype(F32)).astype(BF)
    blocks = []
    for i, da in enumerate((dq, dk, dv)):
        da_ref[i] = da
        grad = da.astype(F32)
        x = jnp.concatenate([halo_ref[i], s_ref[i]], axis=0)
        sums = []
        for j in range(KF):
            sums.append(jnp.sum(grad * dot(sm_ref[j * rows : (j + 1) * rows, :], x), axis=0, keepdims=True))
        sums.append(jnp.zeros_like(sums[0]))
        blocks.append(jnp.concatenate(sums, axis=0))
    result = jnp.concatenate(blocks, axis=0)
    half = pl.num_programs(0) // 2

    @pl.when(step < half)
    def _():
        send_ref[...] = result

    @pl.when(step >= half)
    def _():
        keep_ref[...] = result


def dstreams_kernel(tokens, len_ref, da_ref, rim_ref, taps_ref, out_ref, sm_ref):
    rows = da_ref.shape[1]

    @pl.when(pl.program_id(0) == 0)
    def _():
        reverse_shifts(sm_ref, Layout(len_ref, rows, tokens))

    for i in range(3):
        x = jnp.concatenate([da_ref[i], rim_ref[i]], axis=0)
        out_ref[i] = tap_sum(sm_ref, taps_ref[i], x, rows).astype(BF)


def shares_kernel(keep_ref, recv_ref, own_ref, *share_refs):
    count = len(share_refs) + 1
    shard = own_ref.shape[0]
    for d in range(count):
        at = pl.ds(pl.multiple_of(lax.rem(lax.axis_index("ctx") + d, count) * shard, 8), shard)
        total = keep_ref[at, :] + recv_ref[at, :].astype(F32)
        if d == 0:
            own_ref[...] = total
        else:
            share_refs[d - 1][...] = total.astype(BF)


def finish_kernel(own_ref, feat_ref, *refs):
    count = (len(refs) - 3) // 2 + 1
    shares, feats = refs[: count - 1], refs[count - 1 : 2 * (count - 1)]
    out_ref, out_feat_ref, slot_ref = refs[2 * (count - 1) :]
    total = own_ref[...]
    for share in shares:
        total = total + share[...].astype(F32)
    out_ref[...] = total
    for d, feat in enumerate((feat_ref, *feats)):
        slot_ref[lax.rem(lax.axis_index("ctx") + (count - d), count)] = feat[...].astype(F32)
    total = slot_ref[0]
    for d in range(1, count):
        total = total + slot_ref[d]
    out_feat_ref[...] = total


def joined_kernel(mine_ref, other_ref, feat_ref, other_feat_ref, dfilt_ref, dfeat_ref):
    width = mine_ref.shape[1]
    here = pl.multiple_of(lax.axis_index("sub") * width, 128)
    there = pl.multiple_of((1 - lax.axis_index("sub")) * width, 128)
    for at, filt, feat in ((here, mine_ref, feat_ref), (there, other_ref, other_feat_ref)):
        dfilt_ref[:, pl.ds(at, width)] = filt[...]
        for i in range(3):
            dfeat_ref[i, :, pl.ds(at, width)] = feat[8 * i : 8 * i + KF, :]


def local(streams, feat_taps, long_filter, upstream, score_dir, seg_lengths, list_ids):
    rows, chans = streams.shape[1:]
    segs = seg_lengths.shape[0]
    shard = long_filter.shape[0]
    ring = ("ctx", "sub")
    tokens = rows * lax.axis_size("ctx") * lax.axis_size("sub")
    shards = lax.axis_size("ctx")
    tile = min(512, chans // 2)
    steps = chans // tile
    half = steps // 2
    ahead, behind, own_wave, back = (jnp.asarray(t) for t in half_wave(rows))
    sub = lax.axis_index("sub")
    sub_of = sub.astype(jnp.int32).reshape(1)
    direction = score_dir.reshape(1, chans)

    smem = pl.BlockSpec(memory_space=pltpu.SMEM)
    blk = lambda *shape: pl.BlockSpec((*shape, tile), lambda i: (0,) * len(shape) + (i,))
    whole = lambda *shape: pl.BlockSpec(shape, lambda i: (0,) * len(shape))
    out = lambda shape, dtype: jax.ShapeDtypeStruct(shape, dtype)
    params = pltpu.CompilerParams(vmem_limit_bytes=VMEM_LIMIT, dimension_semantics=("arbitrary",))
    cost = lambda us: pl.CostEstimate(flops=int(us * 1e9), bytes_accessed=int(us * 3e6), transcendentals=0)

    sq_next = passed_along(streams[0], ring, -1)
    halo = passed_along(streams[:, rows - RIM :, :], ring, 1)
    part = lax.dynamic_slice_in_dim(long_filter, sub * (chans // 2), chans // 2, 1)
    mine = jnp.stack([part] + [rotated(part, "ctx", d) for d in range(1, shards)])
    up_next = passed_along(upstream, ring, -1)
    other = swapped(mine, "sub", 1)

    query, key_feat, value_feat, product = pl.pallas_call(
        lambda *refs: feat_kernel(tokens, *refs),
        grid=(steps,),
        in_specs=[smem, blk(3, rows), blk(3, RIM), blk(3, KF)],
        out_specs=[blk(rows)] * 4,
        out_shape=[out((rows, chans), BF)] * 4,
        scratch_shapes=[pltpu.VMEM((KF * rows, rows + RIM), BF)],
        compiler_params=params, cost_estimate=cost(3), name="feats",
    )(seg_lengths, streams, halo, feat_taps)
    z_prev = passed_along(product, ring, 1)

    half_blk = pl.BlockSpec((shards, shard, tile), lambda i: (0, 0, i % half))
    dzq, q_next, spectrum, partial = pl.pallas_call(
        lambda *refs: dzq_kernel(tokens, *refs),
        grid=(steps,),
        in_specs=[smem, pl.BlockSpec((1, RIM, tile), lambda i: (0, rows // RIM - 1, i)), blk(rows), blk(3, KF),
                  half_blk, half_blk, blk(rows), blk(rows), blk(1),
                  whole(2 * rows, 2 * rows), whole(2 * rows, rows), whole(rows, 2 * rows)],
        out_specs=[blk(rows), blk(rows), blk(2 * rows), whole(segs, 128)],
        out_shape=[out((rows, chans), F32), out((rows, chans), BF), out((2 * rows, chans), F32), out((segs, 128), F32)],
        scratch_shapes=[pltpu.VMEM((KF * rows, rows + RIM), BF), pltpu.VMEM((2 * rows, 2 * rows), F32),
                        pltpu.VMEM((rows, 2 * rows), F32), pltpu.VMEM((LH, tile), F32)],
        compiler_params=params, cost_estimate=cost(3), name="adjoint_of_q",
    )(seg_lengths, streams, sq_next, feat_taps, mine, other, query, product, direction, ahead, own_wave, back)

    totals = summed_everywhere(partial)

    mixed = pl.pallas_call(
        lambda *refs: w_kernel(tokens, *refs),
        grid=(steps,),
        in_specs=[smem, blk(rows), blk(rows), blk(2 * rows), whole(2 * rows, 2 * rows), whole(rows, 2 * rows)],
        out_specs=blk(rows),
        out_shape=out((rows, chans), F32),
        scratch_shapes=[pltpu.VMEM((2 * rows, 2 * rows), F32), pltpu.VMEM((rows, 2 * rows), F32)],
        compiler_params=params, cost_estimate=cost(3), name="mixed",
    )(seg_lengths, product, z_prev, spectrum, behind, back)

    dzu = pl.pallas_call(
        lambda *refs: dzu_kernel(tokens, *refs),
        grid=(steps,),
        in_specs=[smem, blk(rows), blk(rows), blk(rows), blk(rows), blk(2 * rows),
                  whole(2 * rows, 2 * rows), whole(rows, 2 * rows)],
        out_specs=blk(rows),
        out_shape=out((rows, chans), F32),
        scratch_shapes=[pltpu.VMEM((2 * rows, 2 * rows), F32), pltpu.VMEM((rows, 2 * rows), F32)],
        compiler_params=params, cost_estimate=cost(3), name="adjoint_of_up",
    )(seg_lengths, query, q_next, upstream, up_next, spectrum, ahead, back)

    turned = lambda i, ref: lax.rem(i + (1 - ref[0]) * half, steps)
    tblk = lambda *shape: pl.BlockSpec((*shape, tile), lambda i, ref: (0,) * len(shape) + (turned(i, ref),))
    twhole = lambda *shape: pl.BlockSpec(shape, lambda i, ref: (0,) * len(shape))
    tsend = lambda *shape: pl.BlockSpec((*shape, tile), lambda i, ref: (0,) * len(shape) + (jnp.minimum(i, half - 1),))
    tkeep = lambda *shape: pl.BlockSpec((*shape, tile), lambda i, ref: (0,) * len(shape) + (jnp.maximum(i - half, 0),))

    f_send, f_keep = pl.pallas_call(
        lambda *refs: dfilter_kernel(tokens, *refs),
        grid_spec=pltpu.PrefetchScalarGridSpec(
            num_scalar_prefetch=1, grid=(steps,),
            in_specs=[smem, smem, twhole(segs, 128)] + [tblk(rows)] * 5 + [tblk(1)]
            + [twhole(2 * rows, 2 * rows), twhole(2 * rows, rows), twhole(rows, 2 * rows)],
            out_specs=[tsend(LH), tkeep(LH)],
            scratch_shapes=[pltpu.VMEM((2 * rows, 2 * rows), F32), pltpu.VMEM((2 * rows, 128), F32),
                            pltpu.VMEM((2 * rows, tile), F32)],
        ),
        out_shape=[out((LH, chans // 2), BF), out((LH, chans // 2), F32)],
        compiler_params=params, cost_estimate=cost(3), name="filter_grad",
    )(sub_of, seg_lengths, list_ids, totals, product, query, q_next, upstream, up_next, direction, ahead, own_wave, back)
    f_recv = swapped(f_send, "sub", 1)

    grads, t_send, t_keep = pl.pallas_call(
        lambda *refs: grads_kernel(tokens, *refs),
        grid_spec=pltpu.PrefetchScalarGridSpec(
            num_scalar_prefetch=1, grid=(steps,),
            in_specs=[smem, smem, twhole(segs, 128), tblk(3, rows), tblk(3, RIM)] + [tblk(rows)] * 4 + [tblk(1)]
            + [tblk(rows)] * 3,
            out_specs=[tblk(3, rows), tsend(24), tkeep(24)],
            scratch_shapes=[pltpu.VMEM((KF * rows, rows + RIM), BF), pltpu.VMEM((rows, 128), F32)],
        ),
        out_shape=[out((3, rows, chans), BF), out((24, chans // 2), F32), out((24, chans // 2), F32)],
        compiler_params=params, cost_estimate=cost(3), name="input_grads",
    )(sub_of, seg_lengths, list_ids, totals, streams, halo, query, key_feat, value_feat, upstream, direction,
      mixed, dzu, dzq)
    rim = passed_along(grads[:, :RIM, :], ring, -1)

    shares = pl.pallas_call(
        shares_kernel,
        out_shape=[out((shard, chans // 2), F32)] + [out((shard, chans // 2), BF)] * (shards - 1),
        compiler_params=pltpu.CompilerParams(vmem_limit_bytes=VMEM_LIMIT), cost_estimate=cost(1), name="filter_shares",
    )(f_keep, f_recv)
    f_parts = [rotated(shares[d], "ctx", d) for d in range(1, shards)]
    t_sum = (t_keep + swapped(t_send, "sub", 1)).astype(BF)
    t_parts = [rotated(t_sum, "ctx", d) for d in range(1, shards)]

    d_streams = pl.pallas_call(
        lambda *refs: dstreams_kernel(tokens, *refs),
        grid=(steps,),
        in_specs=[smem, blk(3, rows), blk(3, RIM), blk(3, KF)],
        out_specs=blk(3, rows),
        out_shape=out((3, rows, chans), BF),
        scratch_shapes=[pltpu.VMEM((KF * rows, rows + RIM), BF)],
        compiler_params=params, cost_estimate=cost(3), name="stream_grads",
    )(seg_lengths, grads, rim, feat_taps)

    f_half, t_half = pl.pallas_call(
        finish_kernel,
        out_shape=[out((shard, chans // 2), F32), out((24, chans // 2), F32)],
        scratch_shapes=[pltpu.VMEM((shards, 24, chans // 2), F32)],
        compiler_params=pltpu.CompilerParams(vmem_limit_bytes=VMEM_LIMIT), cost_estimate=cost(1), name="shard_sums",
    )(shares[0], t_sum, *f_parts, *t_parts)
    d_filter, d_feat = pl.pallas_call(
        joined_kernel,
        out_shape=[out((shard, chans), F32), out((3, KF, chans), F32)],
        compiler_params=pltpu.CompilerParams(vmem_limit_bytes=VMEM_LIMIT), cost_estimate=cost(1), name="both_halves",
    )(f_half, swapped(f_half, "sub", 1), t_half, swapped(t_half, "sub", 1))
    return (d_streams, d_feat, d_filter)


def solution(mesh):
    placed = (
        P(None, ("groups", "ctx", "sub"), "fsdp"),
        P(None, None, "fsdp"),
        P("ctx", "fsdp"),
        P(("groups", "ctx", "sub"), "fsdp"),
        P("fsdp"),
        P("groups"),
        P("groups"),
    )
    return jax.shard_map(
        local,
        mesh=mesh,
        in_specs=placed,
        out_specs=(
            P(None, ("groups", "ctx", "sub"), "fsdp"),
            P("groups", None, "fsdp"),
            P(("groups", "ctx"), "fsdp"),
        ),
        check_vma=False,
    )
```

time: 392 us -> 109 us (0.28)
  the two profiles are of different devices: /device:TPU:0 before, /device:TPU:7 now
where the time goes in v1:
time: 109 us; the launch traced here: 107 us
  Pallas kernels  47 us (43%)
  starting transfers between devices  44.9 us (41%)
  waiting for transfers between devices  10.4 us (10%)
  local copies, waits for them, and re-layouts  3.85 us (4%)
    ppermute x9, starting transfers between devices, swapped(): lax.ppermute(value, axis, [(source, source ^ distance) for source in rang...  17.5 us
    ppermute x5, starting transfers between devices, passed_along(): lax.ppermute(value, axis, [(source, source + steps) for source in range(l...  16.3 us
    ppermute x9, starting transfers between devices, rotated(): lax.ppermute(value, axis, [(source, (source + distance) % count) for sour...  11 us
    pallas_call x1, Pallas kernels, local(): pl.pallas_call(lambda *refs: dzq_kernel(tokens, *refs), grid=(steps,), in...  9.58 us
    pallas_call x1, Pallas kernels, local(): pl.pallas_call(lambda *refs: dfilter_kernel(tokens, *refs), grid_spec=plt...  6.99 us
    pallas_call x1, Pallas kernels, local(): pl.pallas_call(lambda *refs: dzu_kernel(tokens, *refs), grid=(steps,), in...  6.74 us
    pallas_call x1, Pallas kernels, local(): pl.pallas_call(lambda *refs: grads_kernel(tokens, *refs), grid_spec=pltpu...  6.5 us
    pallas_call x1, Pallas kernels, local(): pl.pallas_call(lambda *refs: w_kernel(tokens, *refs), grid=(steps,), in_s...  6.43 us
  transfers between devices with their start and end apart: 23, of which 4 were waited for; matrix products, arithmetic and copies ran while one was open for 1% of the time, Pallas kernels for 31%

profile of v1, /device:TPU:7, one launch (start us, length us, event | category | flops | bytes accessed | tf_op | source)
XLA Modules:
  0.0 107.2 jit_solution(16439175623915601660)
XLA Ops:
  0.6 0.0 copy-start
  0.6 0.0 copy-start.1
  0.7 1.2 %slice_bitcast_fusion = bf16[128,2048]{1,0:T(8,128)(2,1)S(1)} fusion(bf16[3,128,2048]{2,1,0:T(8,128)(2,1)} %refs_4_.2), kind=kLoop, calls=%fused_computation | loop fusion | bytes 1048576 | tf_op jit(solution)/shard_map/squeeze | solution.py:432
  1.9 2.6 %collective-permute-start = (bf16[128,2048]{1,0:T(8,128)(2,1)S(1)}, bf16[128,2048]{1,0:T(8,128)(2,1)S(1)}, u32[]{:S(2)}, u32[]{:S(2)}) collective-permute-start(bf16[128,2048]{1,0:T(8,128)(2,1)S(1)} %slice_bitcast_fusion), channel_id=1, source_target_pairs={{1,0},{4,1},{5,4},{8,5},{9,8},{12,9},{13,12},{3,2},{6,3},{7,6},{10... | collective-permute-start | bytes 1572872 | tf_op jit(solution)/shard_map/ppermute | solution.py:20
  4.5 2.4 %collective-permute-start.2 = (bf16[32,1024]{1,0:T(8,128)(2,1)S(1)}, bf16[32,1024]{1,0:T(8,128)(2,1)S(1)}, u32[]{:S(2)}, u32[]{:S(2)}) collective-permute-start(bf16[32,1024]{1,0:T(8,128)(2,1)S(1)} %constant_dynamic-slice_fusion), channel_id=1, source_target_pairs={{0,8},{4,12},{8,0},{12,4},{1,9},{5,13},{9,1},{13,5},{2,10},{6,14},... | collective-permute-start | bytes 196616 | tf_op jit(solution)/shard_map/ppermute | solution.py:30
  6.9 1.3 %collective-permute-start.1 = (bf16[32,1024]{1,0:T(8,128)(2,1)S(1)}, bf16[32,1024]{1,0:T(8,128)(2,1)S(1)}, u32[]{:S(2)}, u32[]{:S(2)}) collective-permute-start(bf16[32,1024]{1,0:T(8,128)(2,1)S(1)} %constant_dynamic-slice_fusion), channel_id=1, source_target_pairs={{0,4},{4,8},{8,12},{12,0},{1,5},{5,9},{9,13},{13,1},{2,6},{6,10},{... | collective-permute-start | bytes 196616 | tf_op jit(solution)/shard_map/ppermute | solution.py:30
  8.2 1.9 %collective-permute-start.3 = (bf16[32,1024]{1,0:T(8,128)(2,1)S(1)}, bf16[32,1024]{1,0:T(8,128)(2,1)S(1)}, u32[]{:S(2)}, u32[]{:S(2)}) collective-permute-start(bf16[32,1024]{1,0:T(8,128)(2,1)S(1)} %constant_dynamic-slice_fusion), channel_id=1, source_target_pairs={{0,12},{4,0},{8,4},{12,8},{1,13},{5,1},{9,5},{13,9},{2,14},{6,2},{... | collective-permute-start | bytes 196616 | tf_op jit(solution)/shard_map/ppermute | solution.py:30
  10.2 0.9 slice.10
  11.1 2.1 %collective-permute-start.5 = (bf16[3,16,2048]{2,1,0:T(8,128)(2,1)S(1)}, bf16[3,16,2048]{2,1,0:T(8,128)(2,1)S(1)}, u32[]{:S(2)}, u32[]{:S(2)}) collective-permute-start(bf16[3,16,2048]{2,1,0:T(8,128)(2,1)S(1)} %slice.10), channel_id=1, source_target_pairs={{0,1},{1,4},{4,5},{5,8},{8,9},{9,12},{12,13},{2,3},{3,6},{6,7},{7,... | collective-permute-start | bytes 589832 | tf_op jit(solution)/shard_map/ppermute | solution.py:20
  13.3 0.0 collective-permute-done.2
  13.3 7.7 %collective-permute-start.11 = (bf16[128,2048]{1,0:T(8,128)(2,1)}, bf16[128,2048]{1,0:T(8,128)(2,1)S(1)}, u32[]{:S(2)}, u32[]{:S(2)}) collective-permute-start(bf16[128,2048]{1,0:T(8,128)(2,1)} %refs_7_.2), channel_id=1, source_target_pairs={{1,0},{4,1},{5,4},{8,5},{9,8},{12,9},{13,12},{3,2},{6,3},{7,6},{10... | collective-permute-start | bytes 1572872 | tf_op jit(solution)/shard_map/ppermute | solution.py:20
  21.0 0.0 collective-permute-done.1
  21.0 0.0 collective-permute-done.3
  21.1 0.0 copy-start.5
  21.1 0.0 copy-start.8
  21.1 0.0 copy-start.10
  21.1 0.0 copy-start.11
  21.1 0.1 collective-permute-start.4
  21.2 0.0 collective-permute-done.5.refs_2_.refs_5_
  21.3 4.7 %feats.1 = (bf16[128,2048]{1,0:T(8,128)(2,1)S(1)}, bf16[128,2048]{1,0:T(8,128)(2,1)S(1)}, bf16[128,2048]{1,0:T(8,128)(2,1)S(1)}, bf16[128,2048]{1,0:T(8,128)(2,1)S(1)}) custom-call(s32[8]{0:T(128)S(1)} %copy-done.7, bf16[3,128,2048]{2,1,0:T(8,128)(2,1)S(1)} %copy-done.1, bf16[3,16,2048]{2,1,0:T(8,128)(2,1)S(1)} %collective-permute-done.5.refs_2_.refs_5_, ...), custom_call_target="tpu_custom_call" | custom-call | flops 3000000000 | bytes 9000000 | tf_op jit(solution)/shard_map/feats/pallas_call | solution.py:439
  26.0 1.9 %collective-permute-start.10 = (bf16[128,2048]{1,0:T(8,128)(2,1)S(1)}, bf16[128,2048]{1,0:T(8,128)(2,1)S(1)}, u32[]{:S(2)}, u32[]{:S(2)}) collective-permute-start(bf16[128,2048]{1,0:T(8,128)(2,1)S(1)} %get-tuple-element.25.refs_7_.refs_1_.refs_4_), channel_id=1, source_target_pairs={{0,1},{1,4},{4,5},{5,8},{8,9},{9,12},{12,13},{2,3},{3,6},{6,7},{7,... | collective-permute-start | bytes 1572872 | tf_op jit(solution)/shard_map/ppermute | solution.py:20
  27.9 0.0 collective-permute-done.4.refs_5_
  27.9 0.0 collective-permute-done.refs_2_
  28.0 0.0 copy-start.3
  28.0 9.6 %adjoint_of_q.1 = (f32[128,2048]{1,0:T(8,128)S(1)}, bf16[128,2048]{1,0:T(8,128)(2,1)S(1)}, f32[256,2048]{1,0:T(8,128)}, f32[8,128]{1,0:T(8,128)S(1)}) custom-call(s32[8]{0:T(128)S(1)} %copy-done.7, bf16[3,128,2048]{2,1,0:T(8,128)(2,1)S(1)} %copy-done.1, bf16[128,2048]{1,0:T(8,128)(2,1)S(1)} %collective-permute-done.refs_2_, f32[3,7,2048]{2,1,0:T(8,128)S(1)} %copy-done.4, ...), custom_call_target="tpu_custom_call" | custom-call | flops 3000000000 | bytes 9000000 | tf_op jit(solution)/shard_map/adjoint_of_q/pallas_call | solution.py:451
  37.5 2.3 %collective-permute-start.6 = (f32[8,128]{1,0:T(8,128)S(1)}, f32[8,128]{1,0:T(8,128)S(1)}, u32[]{:S(2)}, u32[]{:S(2)}) collective-permute-start(f32[8,128]{1,0:T(8,128)S(1)} %get-tuple-element.26), channel_id=1, source_target_pairs={{0,1},{1,0},{2,3},{3,2},{4,5},{5,4},{6,7},{7,6},{8,9},{9,8},{10,11... | collective-permute-start | bytes 12296 | tf_op jit(solution)/shard_map/ppermute | solution.py:25
  39.9 0.8 collective-permute-done.6
  40.7 0.2 collective-permute-start.7
  41.0 2.2 %collective-permute-done.7 = f32[8,128]{1,0:T(8,128)S(1)} collective-permute-done((f32[8,128]{1,0:T(8,128)S(1)}, f32[8,128]{1,0:T(8,128)S(1)}, u32[]{:S(2)}, u32[]{:S(2)}) %collective-permute-start.7) | collective-permute-done | bytes 4128 | tf_op jit(solution)/shard_map/ppermute | solution.py:25
  43.2 0.0 collective-permute-start.8
  43.2 2.5 %collective-permute-done.8 = f32[8,128]{1,0:T(8,128)S(1)} collective-permute-done((f32[8,128]{1,0:T(8,128)S(1)}, f32[8,128]{1,0:T(8,128)S(1)}, u32[]{:S(2)}, u32[]{:S(2)}) %collective-permute-start.8) | collective-permute-done | bytes 4128 | tf_op jit(solution)/shard_map/ppermute | solution.py:25
  45.6 0.0 collective-permute-start.9
  45.6 0.0 collective-permute-done.11.refs_4_.refs_8_
  45.7 1.6 %copy-done.12 = f32[256,2048]{1,0:T(8,128)S(1)} copy-done((f32[256,2048]{1,0:T(8,128)S(1)}, f32[256,2048]{1,0:T(8,128)}, u32[]{:S(2)}) %copy-start.12) | copy-done | bytes 2097176
  47.3 6.7 %adjoint_of_up.1.refs_12_ = f32[128,2048]{1,0:T(8,128)S(1)} custom-call(s32[8]{0:T(128)S(1)} %copy-done.7, bf16[128,2048]{1,0:T(8,128)(2,1)S(1)} %get-tuple-element.24.refs_6_.refs_1_.refs_5_, bf16[128,2048]{1,0:T(8,128)(2,1)S(1)} %get-tuple-element.30.refs_2_.refs_6_, bf16[128,2048]{1,0:T(8,128)(2,1)S(1)} %copy-done.3, ...), custom_call_target="tpu_custom_call" | custom-call | flops 3000000000 | bytes 9000000 | tf_op jit(solution)/shard_map/adjoint_of_up/pallas_call | solution.py:476
  54.0 0.0 collective-permute-done.9
  54.0 0.0 copy-start.6
  54.0 0.0 collective-permute-done.10.refs_2_
  54.1 6.4 %mixed.1.refs_11_ = f32[128,2048]{1,0:T(8,128)S(1)} custom-call(s32[8]{0:T(128)S(1)} %copy-done.7, bf16[128,2048]{1,0:T(8,128)(2,1)S(1)} %get-tuple-element.25.refs_7_.refs_1_.refs_4_, bf16[128,2048]{1,0:T(8,128)(2,1)S(1)} %collective-permute-done.10.refs_2_, f32[256,2048]{1,0:T(8,128)S(1)} %copy-done.12, f32[256,256]{1,0:T(8,128)S(1)} %copy-done.9, ...), custom_call_target="tpu_custom_call" | custom-call | flops 3000000000 | bytes 9000000 | tf_op jit(solution)/shard_map/mixed/pallas_call | solution.py:466
  60.5 6.5 %input_grads.1 = (bf16[3,128,2048]{2,1,0:T(8,128)(2,1)}, f32[24,1024]{1,0:T(8,128)S(1)}, f32[24,1024]{1,0:T(8,128)S(1)}) custom-call(s32[1]{0:T(128)} %bitcast.refs_0_, s32[8]{0:T(128)S(1)} %copy-done.7, s32[8]{0:T(128)S(1)} %copy-done.6, f32[8,128]{1,0:T(8,128)S(1)} %add.22.refs_3_, bf16[3,128,2048]{2,1,0:T(8,128)(2,1)} %refs_4_.2, ...), custom_call_target="tpu_custom_call" | custom-call | flops 3000000000 | bytes 9000000 | tf_op jit(solution)/shard_map/input_grads/pallas_call | solution.py:508
  67.0 6.2 %collective-permute-start.14 = (f32[24,1024]{1,0:T(8,128)S(1)}, f32[24,1024]{1,0:T(8,128)S(1)}, u32[]{:S(2)}, u32[]{:S(2)}) collective-permute-start(f32[24,1024]{1,0:T(8,128)S(1)} %get-tuple-element.37), channel_id=1, source_target_pairs={{0,1},{1,0},{2,3},{3,2},{4,5},{5,4},{6,7},{7,6},{8,9},{9,8},{10,11... | collective-permute-start | bytes 294920 | tf_op jit(solution)/shard_map/ppermute | solution.py:25
  73.2 7.0 %filter_grad.1 = (bf16[128,1024]{1,0:T(8,128)(2,1)S(1)}, f32[128,1024]{1,0:T(8,128)S(1)}) custom-call(s32[1]{0:T(128)} %bitcast.refs_0_, s32[8]{0:T(128)S(1)} %copy-done.7, s32[8]{0:T(128)S(1)} %copy-done.6, f32[8,128]{1,0:T(8,128)S(1)} %add.22.refs_3_, bf16[128,2048]{1,0:T(8,128)(2,1)S(1)} %get-tuple-element.25.refs_7_.refs_1_.refs_4_, ...), custom_call_target="tpu_custom_call" | custom-call | flops 3000000000 | bytes 9000000 | tf_op jit(solution)/shard_map/filter_grad/pallas_call | solution.py:493
  80.2 1.5 %collective-permute-start.13 = (bf16[128,1024]{1,0:T(8,128)(2,1)S(1)}, bf16[128,1024]{1,0:T(8,128)(2,1)S(1)}, u32[]{:S(2)}, u32[]{:S(2)}) collective-permute-start(bf16[128,1024]{1,0:T(8,128)(2,1)S(1)} %get-tuple-element.34), channel_id=1, source_target_pairs={{0,1},{1,0},{2,3},{3,2},{4,5},{5,4},{6,7},{7,6},{8,9},{9,8},{10,11... | collective-permute-start | bytes 786440 | tf_op jit(solution)/shard_map/ppermute | solution.py:25
  81.7 1.9 %collective-permute-start.12 = (bf16[3,16,2048]{2,1,0:T(8,128)(2,1)S(1)}, bf16[3,16,2048]{2,1,0:T(8,128)(2,1)S(1)}, u32[]{:S(2)}, u32[]{:S(2)}) collective-permute-start(bf16[3,16,2048]{2,1,0:T(8,128)(2,1)S(1)} %slice.11), channel_id=1, source_target_pairs={{1,0},{4,1},{5,4},{8,5},{9,8},{12,9},{13,12},{3,2},{6,3},{7,6},{10... | collective-permute-start | bytes 589832 | tf_op jit(solution)/shard_map/ppermute | solution.py:20
  83.6 0.0 collective-permute-done.14
  83.7 0.1 collective-permute-start.20
  83.7 0.1 collective-permute-start.19
  83.8 0.0 collective-permute-done.13.recv_ref
  83.8 0.1 filter_shares.1
  83.9 1.4 %collective-permute-start.15 = (bf16[32,1024]{1,0:T(8,128)(2,1)S(1)}, bf16[32,1024]{1,0:T(8,128)(2,1)S(1)}, u32[]{:S(2)}, u32[]{:S(2)}) collective-permute-start(bf16[32,1024]{1,0:T(8,128)(2,1)S(1)} %get-tuple-element.38), channel_id=1, source_target_pairs={{0,4},{4,8},{8,12},{12,0},{1,5},{5,9},{9,13},{13,1},{2,6},{6,10},{... | collective-permute-start | bytes 196616 | tf_op jit(solution)/shard_map/ppermute | solution.py:30
  85.3 2.4 %collective-permute-start.16 = (bf16[32,1024]{1,0:T(8,128)(2,1)S(1)}, bf16[32,1024]{1,0:T(8,128)(2,1)S(1)}, u32[]{:S(2)}, u32[]{:S(2)}) collective-permute-start(bf16[32,1024]{1,0:T(8,128)(2,1)S(1)} %get-tuple-element.39), channel_id=1, source_target_pairs={{0,8},{4,12},{8,0},{12,4},{1,9},{5,13},{9,1},{13,5},{2,10},{6,14},... | collective-permute-start | bytes 196616 | tf_op jit(solution)/shard_map/ppermute | solution.py:30
  87.7 0.0 collective-permute-done.20.refs_5_
  87.7 1.0 collective-permute-start.17
  88.7 0.0 collective-permute-done.19.refs_4_
  88.7 0.5 collective-permute-start.18
  89.2 4.9 %collective-permute-done.18.refs_3_ = bf16[24,1024]{1,0:T(8,128)(2,1)S(1)} collective-permute-done((bf16[24,1024]{1,0:T(8,128)(2,1)S(1)}, bf16[24,1024]{1,0:T(8,128)(2,1)S(1)}, u32[]{:S(2)}, u32[]{:S(2)}) %collective-permute-start.18) | collective-permute-done | bytes 49184 | tf_op jit(solution)/shard_map/ppermute | solution.py:30
  94.0 0.1 shard_sums.1
  94.1 7.1 %collective-permute-start.22 = (f32[24,1024]{1,0:T(8,128)S(1)}, f32[24,1024]{1,0:T(8,128)S(1)}, u32[]{:S(2)}, u32[]{:S(2)}) collective-permute-start(f32[24,1024]{1,0:T(8,128)S(1)} %get-tuple-element.42.feat_ref), channel_id=1, source_target_pairs={{0,1},{1,0},{2,3},{3,2},{4,5},{5,4},{6,7},{7,6},{8,9},{9,8},{10,11... | collective-permute-start | bytes 294920 | tf_op jit(solution)/shard_map/ppermute | solution.py:25
  101.3 0.1 collective-permute-start.21
  101.3 0.0 collective-permute-done.12.refs_2_
  101.3 5.1 %stream_grads.1 = bf16[3,128,2048]{2,1,0:T(8,128)(2,1)} custom-call(s32[8]{0:T(128)S(1)} %copy-done.7, bf16[3,128,2048]{2,1,0:T(8,128)(2,1)S(1)} %copy-done.2, bf16[3,16,2048]{2,1,0:T(8,128)(2,1)S(1)} %collective-permute-done.12.refs_2_, f32[3,7,2048]{2,1,0:T(8,128)S(1)} %copy-done.4), custom_call_target="tpu_custom_call" | custom-call | flops 3000000000 | bytes 9000000 | tf_op jit(solution)/shard_map/stream_grads/pallas_call | solution.py:532
  106.4 0.0 collective-permute-done.22.other_feat_ref
  106.4 0.0 collective-permute-done.21.other_ref
  106.4 0.8 both_halves.1
  (29 shorter events, 0.1 us)
Async XLA Ops:
  0.6 3.9 %copy-start = (bf16[32,2048]{1,0:T(8,128)(2,1)S(1)}, bf16[32,2048]{1,0:T(8,128)(2,1)}, u32[]{:S(2)}) copy-start(bf16[32,2048]{1,0:T(8,128)(2,1)} %param.13) | copy-start | bytes 393220
  0.6 20.6 %copy-start.1 = (bf16[3,128,2048]{2,1,0:T(8,128)(2,1)S(1)}, bf16[3,128,2048]{2,1,0:T(8,128)(2,1)}, u32[]{:S(2)}) copy-start(bf16[3,128,2048]{2,1,0:T(8,128)(2,1)} %refs_4_.2) | copy-start | bytes 4718596
  0.7 20.6 %copy-start.7 = (s32[8]{0:T(128)S(1)}, s32[8]{0:T(128)}, u32[]{:S(2)}) copy-start(s32[8]{0:T(128)} %refs_1_.7) | copy-start | bytes 100
  0.7 20.6 %copy-start.4 = (f32[3,7,2048]{2,1,0:T(8,128)S(1)}, f32[3,7,2048]{2,1,0:T(8,128)}, u32[]{:S(2)}) copy-start(f32[3,7,2048]{2,1,0:T(8,128)} %refs_3_.7) | copy-start | bytes 516100
  1.9 26.0 %collective-permute-start = (bf16[128,2048]{1,0:T(8,128)(2,1)S(1)}, bf16[128,2048]{1,0:T(8,128)(2,1)S(1)}, u32[]{:S(2)}, u32[]{:S(2)}) collective-permute-start(bf16[128,2048]{1,0:T(8,128)(2,1)S(1)} %slice_bitcast_fusion), channel_id=1, source_target_pairs={{1,0},{4,1},{5,4},{8,5},{9,8},{12,9},{13,12},{3,2},{6,3},{7,6},{10... | collective-permute-start | bytes 1572872 | tf_op jit(solution)/shard_map/ppermute | solution.py:20
  4.5 8.8 %collective-permute-start.2 = (bf16[32,1024]{1,0:T(8,128)(2,1)S(1)}, bf16[32,1024]{1,0:T(8,128)(2,1)S(1)}, u32[]{:S(2)}, u32[]{:S(2)}) collective-permute-start(bf16[32,1024]{1,0:T(8,128)(2,1)S(1)} %constant_dynamic-slice_fusion), channel_id=1, source_target_pairs={{0,8},{4,12},{8,0},{12,4},{1,9},{5,13},{9,1},{13,5},{2,10},{6,14},... | collective-permute-start | bytes 196616 | tf_op jit(solution)/shard_map/ppermute | solution.py:30
  6.9 14.1 %collective-permute-start.1 = (bf16[32,1024]{1,0:T(8,128)(2,1)S(1)}, bf16[32,1024]{1,0:T(8,128)(2,1)S(1)}, u32[]{:S(2)}, u32[]{:S(2)}) collective-permute-start(bf16[32,1024]{1,0:T(8,128)(2,1)S(1)} %constant_dynamic-slice_fusion), channel_id=1, source_target_pairs={{0,4},{4,8},{8,12},{12,0},{1,5},{5,9},{9,13},{13,1},{2,6},{6,10},{... | collective-permute-start | bytes 196616 | tf_op jit(solution)/shard_map/ppermute | solution.py:30
  8.2 12.8 %collective-permute-start.3 = (bf16[32,1024]{1,0:T(8,128)(2,1)S(1)}, bf16[32,1024]{1,0:T(8,128)(2,1)S(1)}, u32[]{:S(2)}, u32[]{:S(2)}) collective-permute-start(bf16[32,1024]{1,0:T(8,128)(2,1)S(1)} %constant_dynamic-slice_fusion), channel_id=1, source_target_pairs={{0,12},{4,0},{8,4},{12,8},{1,13},{5,1},{9,5},{13,9},{2,14},{6,2},{... | collective-permute-start | bytes 196616 | tf_op jit(solution)/shard_map/ppermute | solution.py:30
  11.1 10.1 %collective-permute-start.5 = (bf16[3,16,2048]{2,1,0:T(8,128)(2,1)S(1)}, bf16[3,16,2048]{2,1,0:T(8,128)(2,1)S(1)}, u32[]{:S(2)}, u32[]{:S(2)}) collective-permute-start(bf16[3,16,2048]{2,1,0:T(8,128)(2,1)S(1)} %slice.10), channel_id=1, source_target_pairs={{0,1},{1,4},{4,5},{5,8},{8,9},{9,12},{12,13},{2,3},{3,6},{6,7},{7,... | collective-permute-start | bytes 589832 | tf_op jit(solution)/shard_map/ppermute | solution.py:20
  13.3 32.4 %collective-permute-start.11 = (bf16[128,2048]{1,0:T(8,128)(2,1)}, bf16[128,2048]{1,0:T(8,128)(2,1)S(1)}, u32[]{:S(2)}, u32[]{:S(2)}) collective-permute-start(bf16[128,2048]{1,0:T(8,128)(2,1)} %refs_7_.2), channel_id=1, source_target_pairs={{1,0},{4,1},{5,4},{8,5},{9,8},{12,9},{13,12},{3,2},{6,3},{7,6},{10... | collective-permute-start | bytes 1572872 | tf_op jit(solution)/shard_map/ppermute | solution.py:20
  21.1 6.8 %copy-start.5 = (f32[2048]{0:T(1024)S(1)}, f32[2048]{0:T(1024)}, u32[]{:S(2)}) copy-start(f32[2048]{0:T(1024)} %param.15) | copy-start | bytes 24580
  21.1 6.8 %copy-start.8 = (f32[256,256]{1,0:T(8,128)S(1)}, f32[256,256]{1,0:T(8,128)}, u32[]{:S(2)}) copy-start(f32[256,256]{1,0:T(8,128)} %constant.18.clone.refs_9_.refs_6_.refs_10_) | copy-start | bytes 786436
  21.1 6.8 %copy-start.10 = (f32[128,256]{1,0:T(8,128)S(1)}, f32[128,256]{1,0:T(8,128)}, u32[]{:S(2)}) copy-start(f32[128,256]{1,0:T(8,128)} %constant.21.clone.refs_11_.refs_5_.refs_7_.refs_12_) | copy-start | bytes 393220
  21.1 6.8 %copy-start.11 = (f32[256,128]{1,0:T(8,128)S(1)}, f32[256,128]{1,0:T(8,128)}, u32[]{:S(2)}) copy-start(f32[256,128]{1,0:T(8,128)} %constant.20.clone.refs_10_.refs_11_) | copy-start | bytes 393220
  21.1 6.8 %collective-permute-start.4 = (bf16[4,32,1024]{2,1,0:T(8,128)(2,1)S(1)}, bf16[4,32,1024]{2,1,0:T(8,128)(2,1)S(1)}, u32[]{:S(2)}, u32[]{:S(2)}) collective-permute-start(bf16[4,32,1024]{2,1,0:T(8,128)(2,1)S(1)} %pad_maximum_fusion.refs_4_), channel_id=1, source_target_pairs={{0,1},{1,0},{2,3},{3,2},{4,5},{5,4},{6,7},{7,6},{8,9},{9,8},{10,11... | collective-permute-start | bytes 786440 | tf_op jit(solution)/shard_map/ppermute | solution.py:25
  26.0 28.1 %collective-permute-start.10 = (bf16[128,2048]{1,0:T(8,128)(2,1)S(1)}, bf16[128,2048]{1,0:T(8,128)(2,1)S(1)}, u32[]{:S(2)}, u32[]{:S(2)}) collective-permute-start(bf16[128,2048]{1,0:T(8,128)(2,1)S(1)} %get-tuple-element.25.refs_7_.refs_1_.refs_4_), channel_id=1, source_target_pairs={{0,1},{1,4},{4,5},{5,8},{8,9},{9,12},{12,13},{2,3},{3,6},{6,7},{7,... | collective-permute-start | bytes 1572872 | tf_op jit(solution)/shard_map/ppermute | solution.py:20
  28.0 17.7 %copy-start.3 = (bf16[128,2048]{1,0:T(8,128)(2,1)S(1)}, bf16[128,2048]{1,0:T(8,128)(2,1)}, u32[]{:S(2)}) copy-start(bf16[128,2048]{1,0:T(8,128)(2,1)} %refs_7_.2) | copy-start | bytes 1572868
  37.5 3.2 %collective-permute-start.6 = (f32[8,128]{1,0:T(8,128)S(1)}, f32[8,128]{1,0:T(8,128)S(1)}, u32[]{:S(2)}, u32[]{:S(2)}) collective-permute-start(f32[8,128]{1,0:T(8,128)S(1)} %get-tuple-element.26), channel_id=1, source_target_pairs={{0,1},{1,0},{2,3},{3,2},{4,5},{5,4},{6,7},{7,6},{8,9},{9,8},{10,11... | collective-permute-start | bytes 12296 | tf_op jit(solution)/shard_map/ppermute | solution.py:25
  40.7 2.5 %collective-permute-start.7 = (f32[8,128]{1,0:T(8,128)S(1)}, f32[8,128]{1,0:T(8,128)S(1)}, u32[]{:S(2)}, u32[]{:S(2)}) collective-permute-start(f32[8,128]{1,0:T(8,128)S(1)} %add.19), channel_id=1, source_target_pairs={{0,2},{2,0},{1,3},{3,1},{4,6},{6,4},{5,7},{7,5},{8,10},{10,8},{9,1... | collective-permute-start | bytes 12296 | tf_op jit(solution)/shard_map/ppermute | solution.py:25
  43.2 2.5 %collective-permute-start.8 = (f32[8,128]{1,0:T(8,128)S(1)}, f32[8,128]{1,0:T(8,128)S(1)}, u32[]{:S(2)}, u32[]{:S(2)}) collective-permute-start(f32[8,128]{1,0:T(8,128)S(1)} %add.20), channel_id=1, source_target_pairs={{0,4},{4,0},{8,12},{12,8},{1,5},{5,1},{9,13},{13,9},{2,6},{6,2},{1... | collective-permute-start | bytes 12296 | tf_op jit(solution)/shard_map/ppermute | solution.py:25
  45.6 8.4 %collective-permute-start.9 = (f32[8,128]{1,0:T(8,128)S(1)}, f32[8,128]{1,0:T(8,128)S(1)}, u32[]{:S(2)}, u32[]{:S(2)}) collective-permute-start(f32[8,128]{1,0:T(8,128)S(1)} %add.21), channel_id=1, source_target_pairs={{0,8},{4,12},{8,0},{12,4},{1,9},{5,13},{9,1},{13,5},{2,10},{6,14},... | collective-permute-start | bytes 12296 | tf_op jit(solution)/shard_map/ppermute | solution.py:25
  45.7 1.6 %copy-start.12 = (f32[256,2048]{1,0:T(8,128)S(1)}, f32[256,2048]{1,0:T(8,128)}, u32[]{:S(2)}) copy-start(f32[256,2048]{1,0:T(8,128)} %get-tuple-element.29.refs_3_.refs_5_) | copy-start | bytes 6291460
  47.3 6.8 %copy-start.9 = (f32[256,256]{1,0:T(8,128)S(1)}, f32[256,256]{1,0:T(8,128)}, u32[]{:S(2)}) copy-start(f32[256,256]{1,0:T(8,128)} %constant.19.clone.refs_4_) | copy-start | bytes 786436
  54.0 6.5 %copy-start.6 = (s32[8]{0:T(128)S(1)}, s32[8]{0:T(128)}, u32[]{:S(2)}) copy-start(s32[8]{0:T(128)} %refs_2_.3) | copy-start | bytes 100
  67.0 14.7 %copy-start.2 = (bf16[3,128,2048]{2,1,0:T(8,128)(2,1)S(1)}, bf16[3,128,2048]{2,1,0:T(8,128)(2,1)}, u32[]{:S(2)}) copy-start(bf16[3,128,2048]{2,1,0:T(8,128)(2,1)} %get-tuple-element.32.refs_1_) | copy-start | bytes 4718596
  67.0 16.6 %collective-permute-start.14 = (f32[24,1024]{1,0:T(8,128)S(1)}, f32[24,1024]{1,0:T(8,128)S(1)}, u32[]{:S(2)}, u32[]{:S(2)}) collective-permute-start(f32[24,1024]{1,0:T(8,128)S(1)} %get-tuple-element.37), channel_id=1, source_target_pairs={{0,1},{1,0},{2,3},{3,2},{4,5},{5,4},{6,7},{7,6},{8,9},{9,8},{10,11... | collective-permute-start | bytes 294920 | tf_op jit(solution)/shard_map/ppermute | solution.py:25
  80.2 3.6 %collective-permute-start.13 = (bf16[128,1024]{1,0:T(8,128)(2,1)S(1)}, bf16[128,1024]{1,0:T(8,128)(2,1)S(1)}, u32[]{:S(2)}, u32[]{:S(2)}) collective-permute-start(bf16[128,1024]{1,0:T(8,128)(2,1)S(1)} %get-tuple-element.34), channel_id=1, source_target_pairs={{0,1},{1,0},{2,3},{3,2},{4,5},{5,4},{6,7},{7,6},{8,9},{9,8},{10,11... | collective-permute-start | bytes 786440 | tf_op jit(solution)/shard_map/ppermute | solution.py:25
  81.7 19.6 %collective-permute-start.12 = (bf16[3,16,2048]{2,1,0:T(8,128)(2,1)S(1)}, bf16[3,16,2048]{2,1,0:T(8,128)(2,1)S(1)}, u32[]{:S(2)}, u32[]{:S(2)}) collective-permute-start(bf16[3,16,2048]{2,1,0:T(8,128)(2,1)S(1)} %slice.11), channel_id=1, source_target_pairs={{1,0},{4,1},{5,4},{8,5},{9,8},{12,9},{13,12},{3,2},{6,3},{7,6},{10... | collective-permute-start | bytes 589832 | tf_op jit(solution)/shard_map/ppermute | solution.py:20
  83.7 4.0 %collective-permute-start.20 = (bf16[24,1024]{1,0:T(8,128)(2,1)S(1)}, bf16[24,1024]{1,0:T(8,128)(2,1)S(1)}, u32[]{:S(2)}, u32[]{:S(2)}) collective-permute-start(bf16[24,1024]{1,0:T(8,128)(2,1)S(1)} %add_convert_fusion.feat_ref), channel_id=1, source_target_pairs={{0,12},{4,0},{8,4},{12,8},{1,13},{5,1},{9,5},{13,9},{2,14},{6,2},{... | collective-permute-start | bytes 147464 | tf_op jit(solution)/shard_map/ppermute | solution.py:30
  83.7 4.9 %collective-permute-start.19 = (bf16[24,1024]{1,0:T(8,128)(2,1)S(1)}, bf16[24,1024]{1,0:T(8,128)(2,1)S(1)}, u32[]{:S(2)}, u32[]{:S(2)}) collective-permute-start(bf16[24,1024]{1,0:T(8,128)(2,1)S(1)} %add_convert_fusion.feat_ref), channel_id=1, source_target_pairs={{0,8},{4,12},{8,0},{12,4},{1,9},{5,13},{9,1},{13,5},{2,10},{6,14},... | collective-permute-start | bytes 147464 | tf_op jit(solution)/shard_map/ppermute | solution.py:30
  83.9 10.1 %collective-permute-start.15 = (bf16[32,1024]{1,0:T(8,128)(2,1)S(1)}, bf16[32,1024]{1,0:T(8,128)(2,1)S(1)}, u32[]{:S(2)}, u32[]{:S(2)}) collective-permute-start(bf16[32,1024]{1,0:T(8,128)(2,1)S(1)} %get-tuple-element.38), channel_id=1, source_target_pairs={{0,4},{4,8},{8,12},{12,0},{1,5},{5,9},{9,13},{13,1},{2,6},{6,10},{... | collective-permute-start | bytes 196616 | tf_op jit(solution)/shard_map/ppermute | solution.py:30
  85.3 8.7 %collective-permute-start.16 = (bf16[32,1024]{1,0:T(8,128)(2,1)S(1)}, bf16[32,1024]{1,0:T(8,128)(2,1)S(1)}, u32[]{:S(2)}, u32[]{:S(2)}) collective-permute-start(bf16[32,1024]{1,0:T(8,128)(2,1)S(1)} %get-tuple-element.39), channel_id=1, source_target_pairs={{0,8},{4,12},{8,0},{12,4},{1,9},{5,13},{9,1},{13,5},{2,10},{6,14},... | collective-permute-start | bytes 196616 | tf_op jit(solution)/shard_map/ppermute | solution.py:30
  87.7 6.4 %collective-permute-start.17 = (bf16[32,1024]{1,0:T(8,128)(2,1)S(1)}, bf16[32,1024]{1,0:T(8,128)(2,1)S(1)}, u32[]{:S(2)}, u32[]{:S(2)}) collective-permute-start(bf16[32,1024]{1,0:T(8,128)(2,1)S(1)} %get-tuple-element.40), channel_id=1, source_target_pairs={{0,12},{4,0},{8,4},{12,8},{1,13},{5,1},{9,5},{13,9},{2,14},{6,2},{... | collective-permute-start | bytes 196616 | tf_op jit(solution)/shard_map/ppermute | solution.py:30
  88.7 5.4 %collective-permute-start.18 = (bf16[24,1024]{1,0:T(8,128)(2,1)S(1)}, bf16[24,1024]{1,0:T(8,128)(2,1)S(1)}, u32[]{:S(2)}, u32[]{:S(2)}) collective-permute-start(bf16[24,1024]{1,0:T(8,128)(2,1)S(1)} %add_convert_fusion.feat_ref), channel_id=1, source_target_pairs={{0,4},{4,8},{8,12},{12,0},{1,5},{5,9},{9,13},{13,1},{2,6},{6,10},{... | collective-permute-start | bytes 147464 | tf_op jit(solution)/shard_map/ppermute | solution.py:30
  94.1 12.3 %collective-permute-start.22 = (f32[24,1024]{1,0:T(8,128)S(1)}, f32[24,1024]{1,0:T(8,128)S(1)}, u32[]{:S(2)}, u32[]{:S(2)}) collective-permute-start(f32[24,1024]{1,0:T(8,128)S(1)} %get-tuple-element.42.feat_ref), channel_id=1, source_target_pairs={{0,1},{1,0},{2,3},{3,2},{4,5},{5,4},{6,7},{7,6},{8,9},{9,8},{10,11... | collective-permute-start | bytes 294920 | tf_op jit(solution)/shard_map/ppermute | solution.py:25
  101.3 5.2 %collective-permute-start.21 = (f32[32,1024]{1,0:T(8,128)S(1)}, f32[32,1024]{1,0:T(8,128)S(1)}, u32[]{:S(2)}, u32[]{:S(2)}) collective-permute-start(f32[32,1024]{1,0:T(8,128)S(1)} %get-tuple-element.41.mine_ref), channel_id=1, source_target_pairs={{0,1},{1,0},{2,3},{3,2},{4,5},{5,4},{6,7},{7,6},{8,9},{9,8},{10,11... | collective-permute-start | bytes 393224 | tf_op jit(solution)/shard_map/ppermute | solution.py:25

commit v2 on v1

v2 whole, which is shorter than its diff:
```python
import jax
import jax.numpy as jnp
import numpy as np
from jax import lax
from jax.experimental import pallas as pl
from jax.experimental.pallas import tpu as pltpu
from jax.sharding import PartitionSpec as P

LH = 128
KF = 7
RIM = 16
FEAT_ROWS = 24
BF = jnp.bfloat16
F32 = jnp.float32
VMEM_LIMIT = 48 * 1024 * 1024


def passed_along(value, axis, steps):
    count = lax.axis_size(axis)
    leading, last = (max(0, -steps), min(count, count - steps))
    return lax.ppermute(value, axis, [(source, source + steps) for source in range(leading, last)])


def swapped(value, axis, distance):
    count = lax.axis_size(axis)
    return lax.ppermute(value, axis, [(source, source ^ distance) for source in range(count)])


def rotated(value, axis, distance):
    count = lax.axis_size(axis)
    return lax.ppermute(value, axis, [(source, (source + distance) % count) for source in range(count)])


def summed_everywhere(value):
    for axis in ("sub", "fsdp", "ctx"):
        distance = 1
        while distance < lax.axis_size(axis):
            value = value + swapped(value, axis, distance)
            distance *= 2
    return value


def half_wave(rows):
    odd = 2 * np.arange(rows)[:, None] + 1
    span = np.arange(-rows, 2 * rows)[None, :]
    angle = np.pi * ((odd * span) % (4 * rows)) / (2 * rows)
    table = np.concatenate([np.cos(angle), -np.sin(angle)], axis=0)
    before, own, after = np.split(table, 3, axis=1)
    back = own.T / rows
    as_f32 = lambda parts: np.concatenate(parts, axis=1).astype(np.float32)
    return as_f32([own, after]), as_f32([own, before]), as_f32([own]), as_f32([back])


def dot(left, right):
    return jnp.dot(left, right, preferred_element_type=F32)


class Layout:
    def __init__(self, len_ref, rows, tokens):
        self.rows, self.tokens = rows, tokens
        self.count = len_ref.shape[0]
        self.base = (lax.axis_index("ctx") * lax.axis_size("sub") + lax.axis_index("sub")) * rows
        offset = jnp.int32(0)
        self.offsets = []
        for s in range(self.count):
            self.offsets.append(offset)
            offset = offset + len_ref[s]

    def segment(self, position):
        seg = jnp.zeros_like(position)
        for s in range(1, self.count):
            seg = seg + jnp.where(position >= self.offsets[s], 1, 0)
        return jnp.where((position >= 0) & (position < self.tokens), seg, -1)

    def age(self, position):
        start = jnp.zeros_like(position)
        for s in range(1, self.count):
            start = jnp.where(position >= self.offsets[s], self.offsets[s], start)
        return position - start

    def scalar_segment(self, position):
        seg = jnp.int32(0)
        for s in range(1, self.count):
            seg = seg + jnp.where(position >= self.offsets[s], 1, 0)
        return seg

    def span(self):
        return self.scalar_segment(self.base), self.scalar_segment(self.base + self.rows - 1) + 1


def causal_shifts(sm_ref, layout, first):
    rows = layout.rows
    row = lax.broadcasted_iota(jnp.int32, (rows, rows + RIM), 0)
    col = lax.broadcasted_iota(jnp.int32, (rows, rows + RIM), 1)
    age = layout.age(layout.base + first + row)
    for j in range(1, KF):
        hit = (col == row + (RIM - j)) & (age >= j)
        sm_ref[(j - 1) * rows : j * rows, :] = jnp.where(hit, 1.0, 0.0).astype(BF)


def reverse_shifts(sm_ref, layout):
    rows = layout.rows
    row = lax.broadcasted_iota(jnp.int32, (rows, rows + RIM), 0)
    col = lax.broadcasted_iota(jnp.int32, (rows, rows + RIM), 1)
    age = layout.age(layout.base + col)
    for j in range(1, KF):
        hit = (col == row + j) & (age >= j)
        sm_ref[(j - 1) * rows : j * rows, :] = jnp.where(hit, 1.0, 0.0).astype(BF)


def tap_sum(sm_ref, taps, here, x, rows):
    total = here.astype(F32) * taps[0:1, :]
    moved = dot(sm_ref[...], x)
    for j in range(1, KF):
        total = total + moved[(j - 1) * rows : j * rows] * taps[j : j + 1, :]
    return total


def feat_kernel(tokens, len_ref, s_ref, halo_ref, taps_ref, q_ref, k_ref, v_ref, z_ref, sm_ref):
    rows = s_ref.shape[1]

    @pl.when(pl.program_id(0) == 0)
    def _():
        causal_shifts(sm_ref, Layout(len_ref, rows, tokens), 0)

    feats = []
    for i, out in enumerate((q_ref, k_ref, v_ref)):
        x = jnp.concatenate([halo_ref[i], s_ref[i]], axis=0)
        feat = tap_sum(sm_ref, taps_ref[i], s_ref[i], x, rows).astype(BF)
        out[...] = feat
        feats.append(feat)
    z_ref[...] = (feats[1].astype(F32) * feats[2].astype(F32)).astype(BF)


def cut_kernel(streams_ref, filter_ref, query_ref, tail_ref, half_ref, sems):
    rows = streams_ref.shape[1]
    width = half_ref.shape[1]
    at = pl.multiple_of(lax.axis_index("sub") * width, 128)
    copies = [
        pltpu.make_async_copy(streams_ref.at[:, pl.ds(rows - RIM, RIM), :], tail_ref, sems.at[0]),
        pltpu.make_async_copy(filter_ref.at[:, pl.ds(at, width)], half_ref, sems.at[1]),
        pltpu.make_async_copy(streams_ref.at[0], query_ref, sems.at[2]),
    ]
    for copy in copies:
        copy.start()
    for copy in copies:
        copy.wait()


def segment_columns(ref, layout, first_own, first_rim):
    rows = layout.rows
    col = lax.broadcasted_iota(jnp.int32, ref.shape, 1)
    position = layout.base + jnp.where(col < rows, col + first_own, col - rows + first_rim)
    ref[...] = layout.segment(position).astype(F32)


def segment_rows(ref, layout):
    row = lax.broadcasted_iota(jnp.int32, ref.shape, 0)
    ref[...] = layout.segment(layout.base + row).astype(F32)


def kept(table, seg_table, s):
    return jnp.where(seg_table == s.astype(F32), table, 0.0).astype(BF)


def times(a, b, rows):
    ar, ai, br, bi = a[:rows], a[rows:], b[:rows], b[rows:]
    return jnp.concatenate([ar * br - ai * bi, ar * bi + ai * br], axis=0)


def conj_times(a, b, rows):
    ar, ai, br, bi = a[:rows], a[rows:], b[:rows], b[rows:]
    return jnp.concatenate([ar * br + ai * bi, ar * bi - ai * br], axis=0)


def spectra_kernel(tokens, len_ref, z_ref, q_ref, up_ref, own_ref, cross_ref, a_ref, segc_ref, slot_ref, sems):
    rows, width = z_ref.shape
    layout = Layout(len_ref, rows, tokens)
    step = pl.program_id(0)
    last = pl.num_programs(0) - 1

    @pl.when(step == 0)
    def _():
        segment_columns(segc_ref, layout, 0, rows)

    u = (q_ref[...].astype(F32) * up_ref[...].astype(F32)).astype(BF)
    a_ref[...] = jnp.zeros_like(a_ref)
    first, end = layout.span()

    def copy(s, at):
        there = cross_ref.at[s, :, pl.ds(pl.multiple_of(at * width, 128), width)]
        return pltpu.make_async_copy(slot_ref.at[s], there, sems.at[s])

    def one_segment(s, carry):
        wave = kept(own_ref[...], segc_ref[...], s)
        z_spec = dot(wave, z_ref[...])
        cross = conj_times(z_spec, dot(wave, q_ref[...]), rows).astype(BF)

        @pl.when(step > 0)
        def _():
            copy(s, step - 1).wait()

        slot_ref[s] = cross
        copy(s, step).start()
        a_ref[...] += conj_times(z_spec, dot(wave, u), rows)
        return carry

    lax.fori_loop(first, end, one_segment, 0)

    @pl.when(step == last)
    def _():
        def settle(s, carry):
            copy(s, step).wait()
            return carry

        lax.fori_loop(first, end, settle, 0)


def cross_copy(cross_ref, slot_ref, sems, s, at, width):
    here = cross_ref.at[s, :, pl.ds(pl.multiple_of(at * width, 128), width)]
    return pltpu.make_async_copy(here, slot_ref.at[s], sems.at[s])


def score_kernel(tokens, len_ref, tail_ref, sqn_ref, taps_ref, mine_ref, other_ref, z_ref, dir_ref, cross_ref,
                 after_ref, own_ref, qn_ref, h_ref, rim_ref, part_ref, sm_ref, segc_ref, filt_ref, slot_ref, sems):
    rows, width = z_ref.shape
    layout = Layout(len_ref, rows, tokens)
    step = pl.program_id(0)
    first, end = layout.span()

    def fetch(s, carry):
        cross_copy(cross_ref, slot_ref, sems, s, step, width).start()
        return carry

    lax.fori_loop(first, end, fetch, 0)

    @pl.when(step == 0)
    def _():
        causal_shifts(sm_ref, layout, rows)
        segment_columns(segc_ref, layout, 0, rows)
        part_ref[...] = jnp.zeros_like(part_ref)

    x = jnp.concatenate([tail_ref[0], sqn_ref[...]], axis=0)
    qn = tap_sum(sm_ref, taps_ref[0], sqn_ref[...], x, rows).astype(BF)
    qn_ref[...] = qn
    shards, shard = mine_ref.shape[0], mine_ref.shape[1]
    half = jnp.where(step < pl.num_programs(0) // 2, 0, 1)
    here = half == lax.axis_index("sub")
    for d in range(shards):
        at = lax.rem(lax.axis_index("ctx") + (shards - d), shards) * shard
        filt_ref[pl.ds(pl.multiple_of(at, 8), shard), :] = jnp.where(here, mine_ref[d].astype(F32), other_ref[d].astype(F32))
    h_ref[...] = dot(own_ref[...].astype(BF), filt_ref[...].astype(BF))
    z_spec = dot(kept(own_ref[...], segc_ref[:, :rows], end - 1), z_ref[...])
    rim = conj_times(z_spec, dot(kept(after_ref[...], segc_ref[:, rows:], end - 1), qn), rows)
    rim_ref[...] = rim.astype(BF)

    def add(s, cross):
        row = jnp.sum(h_ref[...] * cross, axis=0, keepdims=True) * dir_ref[...] * (1.0 / rows)
        lanes = row[:, :128]
        for c in range(128, row.shape[1], 128):
            lanes = lanes + row[:, c : c + 128]
        part_ref[pl.ds(s, 1), :] += lanes

    add(end - 1, rim)

    def one_segment(s, carry):
        cross_copy(cross_ref, slot_ref, sems, s, step, width).wait()
        add(s, slot_ref[s].astype(F32))
        return carry

    lax.fori_loop(first, end, one_segment, 0)


def dzq_kernel(tokens, len_ref, q_ref, qn_ref, h_ref, ahead_ref, back_ref, dzq_ref, segc_ref, segr_ref):
    rows = q_ref.shape[0]
    layout = Layout(len_ref, rows, tokens)

    @pl.when(pl.program_id(0) == 0)
    def _():
        segment_columns(segc_ref, layout, 0, rows)
        segment_rows(segr_ref, layout)

    q_ext = jnp.concatenate([q_ref[...], qn_ref[...]], axis=0)
    dzq_ref[...] = jnp.zeros_like(dzq_ref)
    first, end = layout.span()

    def one_segment(s, carry):
        spectrum = dot(kept(ahead_ref[...], segc_ref[...], s), q_ext)
        g = conj_times(h_ref[...], spectrum, rows).astype(BF)
        dzq_ref[...] += dot(kept(back_ref[...], segr_ref[...], s), g)
        return carry

    lax.fori_loop(first, end, one_segment, 0)


def w_kernel(tokens, len_ref, z_ref, zp_ref, h_ref, behind_ref, back_ref, w_ref, segc_ref, segr_ref):
    rows = z_ref.shape[0]
    layout = Layout(len_ref, rows, tokens)

    @pl.when(pl.program_id(0) == 0)
    def _():
        segment_columns(segc_ref, layout, 0, -rows)
        segment_rows(segr_ref, layout)

    z_ext = jnp.concatenate([z_ref[...], zp_ref[...]], axis=0)
    w_ref[...] = jnp.zeros_like(w_ref)
    first, end = layout.span()

    def one_segment(s, carry):
        spectrum = dot(kept(behind_ref[...], segc_ref[...], s), z_ext)
        g = times(h_ref[...], spectrum, rows).astype(BF)
        w_ref[...] += dot(kept(back_ref[...], segr_ref[...], s), g)
        return carry

    lax.fori_loop(first, end, one_segment, 0)


def dzu_kernel(tokens, len_ref, q_ref, qn_ref, up_ref, upn_ref, h_ref, z_ref, a_ref, ahead_ref, own_ref, back_ref,
               dzu_ref, total_ref, segc_ref, segr_ref):
    rows = q_ref.shape[0]
    layout = Layout(len_ref, rows, tokens)

    @pl.when(pl.program_id(0) == 0)
    def _():
        segment_columns(segc_ref, layout, 0, rows)
        segment_rows(segr_ref, layout)

    own = (q_ref[...].astype(F32) * up_ref[...].astype(F32)).astype(BF)
    rim = (qn_ref[...].astype(F32) * upn_ref[...].astype(F32)).astype(BF)
    u_ext = jnp.concatenate([own, rim], axis=0)
    dzu_ref[...] = jnp.zeros_like(dzu_ref)
    first, end = layout.span()
    z_spec = dot(kept(own_ref[...], segc_ref[:, :rows], end - 1), z_ref[...])
    rim_spec = dot(kept(ahead_ref[:, rows:], segc_ref[:, rows:], end - 1), rim)
    total_ref[...] = a_ref[...] + conj_times(z_spec, rim_spec, rows)

    def one_segment(s, carry):
        spectrum = dot(kept(ahead_ref[...], segc_ref[...], s), u_ext)
        g = conj_times(h_ref[...], spectrum, rows).astype(BF)
        dzu_ref[...] += dot(kept(back_ref[...], segr_ref[...], s), g)
        return carry

    lax.fori_loop(first, end, one_segment, 0)


def coefficients(len_ref, ids_ref, part_ref):
    count = len_ref.shape[0]
    index = lax.broadcasted_iota(jnp.int32, (count, 128), 0)
    length = jnp.zeros((count, 128), F32)
    ids = jnp.zeros((count, 128), jnp.int32)
    for s in range(count):
        length = jnp.where(index == s, len_ref[s].astype(F32), length)
        ids = jnp.where(index == s, ids_ref[s], ids)
    scores = jnp.broadcast_to(jnp.sum(part_ref[...], axis=1, keepdims=True), (count, 128)) / length
    total = jnp.zeros((count, 128), F32)
    mates = jnp.zeros((count, 128), F32)
    for s in range(count):
        same = jnp.where(ids == ids_ref[s], 1.0, 0.0)
        mates = mates + same
        total = total + same * scores[s : s + 1, :]
    return (scores - total / mates) / length


def token_coefficients(coef, seg):
    spread = jnp.zeros(seg.shape, F32)
    for s in range(coef.shape[0]):
        spread = jnp.where(seg == s, coef[s : s + 1, :], spread)
    return spread


def across(column, width):
    return jnp.concatenate([column] * (width // 128), axis=1)


def grads_kernel(tokens, sub_ref, len_ref, ids_ref, part_ref, s_ref, halo_ref, q_ref, k_ref, v_ref, up_ref, dir_ref,
                 w_ref, dzu_ref, dzq_ref, a_ref, rim_ref, cross_ref, back_ref,
                 da_ref, head_ref, send_ref, keep_ref, sm_ref, coef_ref, tok_ref, acc_ref, slot_ref, sems):
    rows, width = q_ref.shape
    layout = Layout(len_ref, rows, tokens)
    step = pl.program_id(0)
    steps = pl.num_programs(0)
    half = steps // 2
    at = lax.rem(step + (1 - sub_ref[0]) * half, steps)
    first, end = layout.span()

    def fetch(s, carry):
        cross_copy(cross_ref, slot_ref, sems, s, at, width).start()
        return carry

    lax.fori_loop(first, end, fetch, 0)

    @pl.when(step == 0)
    def _():
        causal_shifts(sm_ref, layout, 0)
        coef = coefficients(len_ref, ids_ref, part_ref)
        coef_ref[...] = coef
        position = layout.base + lax.broadcasted_iota(jnp.int32, (rows, 128), 0)
        tok_ref[...] = token_coefficients(coef, layout.segment(position))

    rise = across(tok_ref[...], width) * dir_ref[...]
    dz = dzu_ref[...] + rise * dzq_ref[...]
    dq = ((up_ref[...].astype(F32) + rise) * w_ref[...]).astype(BF)
    dk = (dz * v_ref[...].astype(F32)).astype(BF)
    dv = (dz * k_ref[...].astype(F32)).astype(BF)
    blocks = []
    for i, da in enumerate((dq, dk, dv)):
        da_ref[i] = da
        head_ref[i] = da[:RIM]
        grad = da.astype(F32)
        x = jnp.concatenate([halo_ref[i], s_ref[i]], axis=0)
        moved = dot(sm_ref[...], x)
        sums = [jnp.sum(grad * s_ref[i].astype(F32), axis=0, keepdims=True)]
        for j in range(1, KF):
            sums.append(jnp.sum(grad * moved[(j - 1) * rows : j * rows], axis=0, keepdims=True))
        sums.append(jnp.zeros_like(sums[0]))
        blocks.append(jnp.concatenate(sums, axis=0))

    def weight(s):
        return across(coef_ref[pl.ds(s, 1), :], width) * dir_ref[...]

    acc_ref[...] = a_ref[...] + weight(end - 1) * rim_ref[...].astype(F32)

    def one_segment(s, carry):
        cross_copy(cross_ref, slot_ref, sems, s, at, width).wait()
        acc_ref[...] += weight(s) * slot_ref[s].astype(F32)
        return carry

    lax.fori_loop(first, end, one_segment, 0)
    result = jnp.concatenate([dot(back_ref[...].astype(BF), acc_ref[...].astype(BF))] + blocks, axis=0)

    @pl.when(step < half)
    def _():
        send_ref[...] = result.astype(BF)

    @pl.when(step >= half)
    def _():
        keep_ref[...] = result


def dstreams_kernel(tokens, len_ref, da_ref, rim_ref, taps_ref, out_ref, sm_ref):
    rows = da_ref.shape[1]

    @pl.when(pl.program_id(0) == 0)
    def _():
        reverse_shifts(sm_ref, Layout(len_ref, rows, tokens))

    for i in range(3):
        x = jnp.concatenate([da_ref[i], rim_ref[i]], axis=0)
        out_ref[i] = tap_sum(sm_ref, taps_ref[i], da_ref[i], x, rows).astype(BF)


def shares_kernel(keep_ref, recv_ref, own_ref, *share_refs):
    count = len(share_refs) + 1
    shard = own_ref.shape[0] - FEAT_ROWS
    taps = keep_ref.shape[0] - FEAT_ROWS
    feat = (keep_ref[taps:, :] + recv_ref[taps:, :].astype(F32)).astype(BF)
    for d in range(count):
        at = pl.ds(pl.multiple_of(lax.rem(lax.axis_index("ctx") + d, count) * shard, 8), shard)
        total = keep_ref[at, :] + recv_ref[at, :].astype(F32)
        ref = own_ref if d == 0 else share_refs[d - 1]
        ref[:shard, :] = total.astype(ref.dtype)
        ref[shard:, :] = feat.astype(ref.dtype)


def finish_kernel(own_ref, *refs):
    shares, (out_ref, slot_ref) = refs[:-2], refs[-2:]
    count = len(shares) + 1
    shard = own_ref.shape[0] - FEAT_ROWS
    total = own_ref[:shard, :]
    for share in shares:
        total = total + share[:shard, :].astype(F32)
    out_ref[:shard, :] = total
    for d, share in enumerate((own_ref, *shares)):
        slot_ref[lax.rem(lax.axis_index("ctx") + (count - d), count)] = share[shard:, :].astype(F32)
    total = slot_ref[0]
    for d in range(1, count):
        total = total + slot_ref[d]
    out_ref[shard:, :] = total


def joined_kernel(mine_ref, other_ref, dfilt_ref, dfeat_ref):
    shard, width = dfilt_ref.shape[0], mine_ref.shape[1]
    here = pl.multiple_of(lax.axis_index("sub") * width, 128)
    there = pl.multiple_of((1 - lax.axis_index("sub")) * width, 128)
    for at, half in ((here, mine_ref), (there, other_ref)):
        dfilt_ref[:, pl.ds(at, width)] = half[:shard, :]
        for i in range(3):
            dfeat_ref[i, :, pl.ds(at, width)] = half[shard + 8 * i : shard + 8 * i + KF, :]


def local(streams, feat_taps, long_filter, upstream, score_dir, seg_lengths, list_ids):
    rows, chans = streams.shape[1:]
    segs = seg_lengths.shape[0]
    shard = long_filter.shape[0]
    ring = ("ctx", "sub")
    tokens = rows * lax.axis_size("ctx") * lax.axis_size("sub")
    shards = lax.axis_size("ctx")
    tile = min(512, chans // 2)
    steps = chans // tile
    half = steps // 2
    ahead, behind, own_wave, back = half_wave(rows)
    after = ahead[:, rows:]
    ahead, behind, own_wave, back, after = (jnp.asarray(t) for t in (ahead, behind, own_wave, back, after))
    sub_of = lax.axis_index("sub").astype(jnp.int32).reshape(1)
    direction = score_dir.reshape(1, chans)

    smem = pl.BlockSpec(memory_space=pltpu.SMEM)
    anywhere = pl.BlockSpec(memory_space=pl.ANY)
    blk = lambda *shape: pl.BlockSpec((*shape, tile), lambda i: (0,) * len(shape) + (i,))
    whole = lambda *shape: pl.BlockSpec(shape, lambda i: (0,) * len(shape))
    out = lambda dtype, *shape: jax.ShapeDtypeStruct(shape, dtype)
    vmem = lambda dtype, *shape: pltpu.VMEM(shape, dtype)
    params = pltpu.CompilerParams(vmem_limit_bytes=VMEM_LIMIT)
    cost = lambda us: pl.CostEstimate(flops=int(us * 1e9), bytes_accessed=int(us * 3e6), transcendentals=0)
    shifts = vmem(BF, (KF - 1) * rows, rows + RIM)
    wide, tall = vmem(F32, 2 * rows, 2 * rows), vmem(F32, rows, 2 * rows)

    sq, tails, part = pl.pallas_call(
        cut_kernel,
        in_specs=[anywhere, anywhere], out_specs=[anywhere] * 3,
        out_shape=[out(BF, rows, chans), out(BF, 3, RIM, chans), out(BF, shard, chans // 2)],
        scratch_shapes=[pltpu.SemaphoreType.DMA((3,))],
        compiler_params=params, cost_estimate=cost(1), name="cut",
    )(streams, long_filter)
    halo = passed_along(tails, ring, 1)
    mine = jnp.stack([part] + [rotated(part, "ctx", d) for d in range(1, shards)])
    sq_next = passed_along(sq, ring, -1)

    query, key_feat, value_feat, product = pl.pallas_call(
        lambda *refs: feat_kernel(tokens, *refs),
        grid=(steps,),
        in_specs=[smem, blk(3, rows), blk(3, RIM), blk(3, KF)],
        out_specs=[blk(rows)] * 4,
        out_shape=[out(BF, rows, chans)] * 4,
        scratch_shapes=[shifts],
        compiler_params=params, cost_estimate=cost(3), name="feats",
    )(seg_lengths, streams, halo, feat_taps)
    z_prev = passed_along(product, ring, 1)

    cross, a_own = pl.pallas_call(
        lambda *refs: spectra_kernel(tokens, *refs),
        grid=(steps,),
        in_specs=[smem, blk(rows), blk(rows), blk(rows), whole(2 * rows, rows)],
        out_specs=[anywhere, blk(2 * rows)],
        out_shape=[out(BF, segs, 2 * rows, chans), out(F32, 2 * rows, chans)],
        scratch_shapes=[vmem(F32, 2 * rows, rows), vmem(BF, segs, 2 * rows, tile), pltpu.SemaphoreType.DMA((segs,))],
        compiler_params=params, cost_estimate=cost(6), name="own_spectra",
    )(seg_lengths, product, query, upstream, own_wave)

    other = swapped(mine, "sub", 1)
    up_held, _ = lax.optimization_barrier((upstream, mine))
    up_next = passed_along(up_held, ring, -1)

    half_blk = pl.BlockSpec((shards, shard, tile), lambda i: (0, 0, i % half))
    q_next, spectrum, rim_cross, partial = pl.pallas_call(
        lambda *refs: score_kernel(tokens, *refs),
        grid=(steps,),
        in_specs=[smem, pl.BlockSpec((1, RIM, tile), lambda i: (0, rows // RIM - 1, i)), blk(rows), blk(3, KF),
                  half_blk, half_blk, blk(rows), blk(1), anywhere, whole(2 * rows, rows), whole(2 * rows, rows)],
        out_specs=[blk(rows), blk(2 * rows), blk(2 * rows), whole(segs, 128)],
        out_shape=[out(BF, rows, chans), out(F32, 2 * rows, chans), out(BF, 2 * rows, chans), out(F32, segs, 128)],
        scratch_shapes=[shifts, wide, vmem(F32, LH, tile), vmem(BF, segs, 2 * rows, tile), pltpu.SemaphoreType.DMA((segs,))],
        compiler_params=params, cost_estimate=cost(3), name="scores",
    )(seg_lengths, streams, sq_next, feat_taps, mine, other, product, direction, cross, after, own_wave)

    totals = summed_everywhere(partial)

    dzq = pl.pallas_call(
        lambda *refs: dzq_kernel(tokens, *refs),
        grid=(steps,),
        in_specs=[smem, blk(rows), blk(rows), blk(2 * rows), whole(2 * rows, 2 * rows), whole(rows, 2 * rows)],
        out_specs=blk(rows),
        out_shape=out(F32, rows, chans),
        scratch_shapes=[wide, tall],
        compiler_params=params, cost_estimate=cost(3), name="adjoint_of_q",
    )(seg_lengths, query, q_next, spectrum, ahead, back)

    mixed = pl.pallas_call(
        lambda *refs: w_kernel(tokens, *refs),
        grid=(steps,),
        in_specs=[smem, blk(rows), blk(rows), blk(2 * rows), whole(2 * rows, 2 * rows), whole(rows, 2 * rows)],
        out_specs=blk(rows),
        out_shape=out(F32, rows, chans),
        scratch_shapes=[wide, tall],
        compiler_params=params, cost_estimate=cost(3), name="mixed",
    )(seg_lengths, product, z_prev, spectrum, behind, back)

    dzu, a_total = pl.pallas_call(
        lambda *refs: dzu_kernel(tokens, *refs),
        grid=(steps,),
        in_specs=[smem, blk(rows), blk(rows), blk(rows), blk(rows), blk(2 * rows), blk(rows), blk(2 * rows),
                  whole(2 * rows, 2 * rows), whole(2 * rows, rows), whole(rows, 2 * rows)],
        out_specs=[blk(rows), blk(2 * rows)],
        out_shape=[out(F32, rows, chans), out(F32, 2 * rows, chans)],
        scratch_shapes=[wide, tall],
        compiler_params=params, cost_estimate=cost(4), name="adjoint_of_up",
    )(seg_lengths, query, q_next, upstream, up_next, spectrum, product, a_own, ahead, own_wave, back)

    turned = lambda i, ref: lax.rem(i + (1 - ref[0]) * half, steps)
    tblk = lambda *shape: pl.BlockSpec((*shape, tile), lambda i, ref: (0,) * len(shape) + (turned(i, ref),))
    twhole = lambda *shape: pl.BlockSpec(shape, lambda i, ref: (0,) * len(shape))
    tsend = lambda *shape: pl.BlockSpec((*shape, tile), lambda i, ref: (0,) * len(shape) + (jnp.minimum(i, half - 1),))
    tkeep = lambda *shape: pl.BlockSpec((*shape, tile), lambda i, ref: (0,) * len(shape) + (jnp.maximum(i - half, 0),))

    grads, heads, send, keep = pl.pallas_call(
        lambda *refs: grads_kernel(tokens, *refs),
        grid_spec=pltpu.PrefetchScalarGridSpec(
            num_scalar_prefetch=1, grid=(steps,),
            in_specs=[smem, smem, twhole(segs, 128), tblk(3, rows), tblk(3, RIM)] + [tblk(rows)] * 4 + [tblk(1)]
            + [tblk(rows)] * 3 + [tblk(2 * rows)] * 2 + [anywhere, twhole(rows, 2 * rows)],
            out_specs=[tblk(3, rows), tblk(3, RIM), tsend(LH + FEAT_ROWS), tkeep(LH + FEAT_ROWS)],
            scratch_shapes=[shifts, vmem(F32, segs, 128), vmem(F32, rows, 128), vmem(F32, 2 * rows, tile),
                            vmem(BF, segs, 2 * rows, tile), pltpu.SemaphoreType.DMA((segs,))],
        ),
        out_shape=[out(BF, 3, rows, chans), out(BF, 3, RIM, chans), out(BF, LH + FEAT_ROWS, chans // 2),
                   out(F32, LH + FEAT_ROWS, chans // 2)],
        compiler_params=params, cost_estimate=cost(5), name="gradients",
    )(sub_of, seg_lengths, list_ids, totals, streams, halo, query, key_feat, value_feat, upstream, direction,
      mixed, dzu, dzq, a_total, rim_cross, cross, back)
    received = swapped(send, "sub", 1)
    shares = pl.pallas_call(
        shares_kernel,
        out_shape=[out(F32, shard + FEAT_ROWS, chans // 2)] + [out(BF, shard + FEAT_ROWS, chans // 2)] * (shards - 1),
        compiler_params=params, cost_estimate=cost(1), name="shares",
    )(keep, received)
    parts = [rotated(shares[d], "ctx", d) for d in range(1, shards)]
    rim = passed_along(heads, ring, -1)

    d_streams = pl.pallas_call(
        lambda *refs: dstreams_kernel(tokens, *refs),
        grid=(steps,),
        in_specs=[smem, blk(3, rows), blk(3, RIM), blk(3, KF)],
        out_specs=blk(3, rows),
        out_shape=out(BF, 3, rows, chans),
        scratch_shapes=[shifts],
        compiler_params=params, cost_estimate=cost(4), name="stream_grads",
    )(seg_lengths, grads, rim, feat_taps)

    summed = pl.pallas_call(
        finish_kernel,
        out_shape=out(F32, shard + FEAT_ROWS, chans // 2),
        scratch_shapes=[vmem(F32, shards, FEAT_ROWS, chans // 2)],
        compiler_params=params, cost_estimate=cost(1), name="shard_sums",
    )(*shares[:1], *parts)
    d_filter, d_feat = pl.pallas_call(
        joined_kernel,
        out_shape=[out(F32, shard, chans), out(F32, 3, KF, chans)],
        compiler_params=params, cost_estimate=cost(1), name="both_halves",
    )(summed, swapped(summed, "sub", 1))
    return (d_streams, d_feat, d_filter)


def solution(mesh):
    placed = (
        P(None, ("groups", "ctx", "sub"), "fsdp"),
        P(None, None, "fsdp"),
        P("ctx", "fsdp"),
        P(("groups", "ctx", "sub"), "fsdp"),
        P("fsdp"),
        P("groups"),
        P("groups"),
    )
    return jax.shard_map(
        local,
        mesh=mesh,
        in_specs=placed,
        out_specs=(
            P(None, ("groups", "ctx", "sub"), "fsdp"),
            P("groups", None, "fsdp"),
            P(("groups", "ctx"), "fsdp"),
        ),
        check_vma=False,
    )
```

time: 109 us -> 116 us (1.064)
  the two profiles are of different devices: /device:TPU:7 before, /device:TPU:0 now
where the time goes in v2:
time: 116 us; the launch traced here: 115 us
  Pallas kernels  66 us (57%)
  starting transfers between devices  21.1 us (18%)
  waiting for transfers between devices  16.7 us (14%)
  local copies, waits for them, and re-layouts  9.21 us (8%)
    pallas_call x1, Pallas kernels, local(): pl.pallas_call(lambda *refs: dzu_kernel(tokens, *refs), grid=(steps,), in...  11.2 us
    pallas_call x1, Pallas kernels, local(): pl.pallas_call(lambda *refs: spectra_kernel(tokens, *refs), grid=(steps,)...  11.2 us
    ppermute x6, starting transfers between devices, rotated(): lax.ppermute(value, axis, [(source, (source + distance) % count) for sour...  10.4 us
    pallas_call x1, Pallas kernels, local(): pl.pallas_call(lambda *refs: grads_kernel(tokens, *refs), grid_spec=pltpu...  9.99 us
    ppermute x6, waiting for transfers between devices, rotated(): lax.ppermute(value, axis, [(source, (source + distance) % count) for sour...  9.37 us
    unnamed x46, local copies, waits for them, and re-layouts  9.21 us
    pallas_call x1, Pallas kernels, local(): pl.pallas_call(lambda *refs: w_kernel(tokens, *refs), grid=(steps,), in_s...  8.08 us
    pallas_call x1, Pallas kernels, local(): pl.pallas_call(lambda *refs: dzq_kernel(tokens, *refs), grid=(steps,), in...  8.03 us
  transfers between devices with their start and end apart: 18, of which 7 were waited for; matrix products, arithmetic and copies ran while one was open for 1% of the time, Pallas kernels for 41%

profile of v2, /device:TPU:0, one launch (start us, length us, event | category | flops | bytes accessed | tf_op | source)
XLA Modules:
  0.0 114.7 jit_solution(6908397780839579582)
XLA Ops:
  0.6 0.0 copy-start
  0.6 1.4 %copy-done = bf16[3,128,2048]{2,1,0:T(8,128)(2,1)S(1)} copy-done((bf16[3,128,2048]{2,1,0:T(8,128)(2,1)S(1)}, bf16[3,128,2048]{2,1,0:T(8,128)(2,1)}, u32[]{:S(2)}) %copy-start) | copy-done | bytes 1572888
  2.0 0.9 copy-done.19
  3.0 0.2 cut.1
  3.1 2.5 %collective-permute-start.5 = (bf16[3,16,2048]{2,1,0:T(8,128)(2,1)S(1)}, bf16[3,16,2048]{2,1,0:T(8,128)(2,1)S(1)}, u32[]{:S(2)}, u32[]{:S(2)}) collective-permute-start(bf16[3,16,2048]{2,1,0:T(8,128)(2,1)S(1)} %get-tuple-element.31), channel_id=1, source_target_pairs={{0,1},{1,4},{4,5},{5,8},{8,9},{9,12},{12,13},{2,3},{3,6},{6,7},{7,... | collective-permute-start | bytes 589832 | tf_op jit(solution)/shard_map/ppermute | solution.py:21
  5.6 2.6 %collective-permute-start.1 = (bf16[32,1024]{1,0:T(8,128)(2,1)S(1)}, bf16[32,1024]{1,0:T(8,128)(2,1)S(1)}, u32[]{:S(2)}, u32[]{:S(2)}) collective-permute-start(bf16[32,1024]{1,0:T(8,128)(2,1)S(1)} %get-tuple-element.30), channel_id=1, source_target_pairs={{0,4},{4,8},{8,12},{12,0},{1,5},{5,9},{9,13},{13,1},{2,6},{6,10},{... | collective-permute-start | bytes 196616 | tf_op jit(solution)/shard_map/ppermute | solution.py:31
  8.3 2.6 %collective-permute-start.2 = (bf16[32,1024]{1,0:T(8,128)(2,1)S(1)}, bf16[32,1024]{1,0:T(8,128)(2,1)S(1)}, u32[]{:S(2)}, u32[]{:S(2)}) collective-permute-start(bf16[32,1024]{1,0:T(8,128)(2,1)S(1)} %get-tuple-element.30), channel_id=1, source_target_pairs={{0,8},{4,12},{8,0},{12,4},{1,9},{5,13},{9,1},{13,5},{2,10},{6,14},... | collective-permute-start | bytes 196616 | tf_op jit(solution)/shard_map/ppermute | solution.py:31
  10.9 1.3 %collective-permute-start.3 = (bf16[32,1024]{1,0:T(8,128)(2,1)S(1)}, bf16[32,1024]{1,0:T(8,128)(2,1)S(1)}, u32[]{:S(2)}, u32[]{:S(2)}) collective-permute-start(bf16[32,1024]{1,0:T(8,128)(2,1)S(1)} %get-tuple-element.30), channel_id=1, source_target_pairs={{0,12},{4,0},{8,4},{12,8},{1,13},{5,1},{9,5},{13,9},{2,14},{6,2},{... | collective-permute-start | bytes 196616 | tf_op jit(solution)/shard_map/ppermute | solution.py:31
  12.2 1.3 %collective-permute-start = (bf16[128,2048]{1,0:T(8,128)(2,1)S(1)}, bf16[128,2048]{1,0:T(8,128)(2,1)S(1)}, u32[]{:S(2)}, u32[]{:S(2)}) collective-permute-start(bf16[128,2048]{1,0:T(8,128)(2,1)S(1)} %get-tuple-element.29), channel_id=1, source_target_pairs={{1,0},{4,1},{5,4},{8,5},{9,8},{12,9},{13,12},{3,2},{6,3},{7,6},{10... | collective-permute-start | bytes 1572872 | tf_op jit(solution)/shard_map/ppermute | solution.py:21
  13.5 0.0 collective-permute-done.1
  13.5 2.6 %collective-permute-done.2 = bf16[32,1024]{1,0:T(8,128)(2,1)S(1)} collective-permute-done((bf16[32,1024]{1,0:T(8,128)(2,1)S(1)}, bf16[32,1024]{1,0:T(8,128)(2,1)S(1)}, u32[]{:S(2)}, u32[]{:S(2)}) %collective-permute-start.2) | collective-permute-done | bytes 65568 | tf_op jit(solution)/shard_map/ppermute | solution.py:31
  16.2 0.0 copy-start.9
  16.2 0.2 collective-permute-start.4
  16.3 1.3 %collective-permute-start.11 = (bf16[128,2048]{1,0:T(8,128)(2,1)S(1)}, bf16[128,2048]{1,0:T(8,128)(2,1)S(1)}, u32[]{:S(2)}, u32[]{:S(2)}) collective-permute-start(bf16[128,2048]{1,0:T(8,128)(2,1)S(1)} %copy-done.4), channel_id=1, source_target_pairs={{1,0},{4,1},{5,4},{8,5},{9,8},{12,9},{13,12},{3,2},{6,3},{7,6},{10... | collective-permute-start | bytes 1572872 | tf_op jit(solution)/shard_map/ppermute | solution.py:21
  17.6 0.0 collective-permute-done.5.refs_2_.refs_5_
  17.7 4.3 %feats.1 = (bf16[128,2048]{1,0:T(8,128)(2,1)S(1)}, bf16[128,2048]{1,0:T(8,128)(2,1)S(1)}, bf16[128,2048]{1,0:T(8,128)(2,1)S(1)}, bf16[128,2048]{1,0:T(8,128)(2,1)S(1)}) custom-call(s32[8]{0:T(128)S(1)} %copy-done.12, bf16[3,128,2048]{2,1,0:T(8,128)(2,1)S(1)} %copy-done, bf16[3,16,2048]{2,1,0:T(8,128)(2,1)S(1)} %collective-permute-done.5.refs_2_.refs_5_, ...), custom_call_target="tpu_custom_call" | custom-call | flops 3000000000 | bytes 9000000 | tf_op jit(solution)/shard_map/feats/pallas_call | solution.py:529
  22.0 0.0 copy-start.5
  22.0 0.0 copy-start.1
  22.0 0.0 copy-start.10
  22.0 0.0 copy-start.11
  22.0 11.2 %own_spectra.1 = (bf16[8,256,2048]{2,1,0:T(8,128)(2,1)}, f32[256,2048]{1,0:T(8,128)S(1)}) custom-call(s32[8]{0:T(128)S(1)} %copy-done.12, bf16[128,2048]{1,0:T(8,128)(2,1)S(1)} %get-tuple-element.32.refs_1_.refs_6_, bf16[128,2048]{1,0:T(8,128)(2,1)S(1)} %get-tuple-element.33.refs_2_.refs_1_.refs_6_, bf16[128,2048]{1,0:T(8,128)(2,1)S(1)} %copy-done.4, ...), custom_call_target="tpu_custom_call" | custom-call | flops 6000000000 | bytes 18000000 | tf_op jit(solution)/shard_map/own_spectra/pallas_call | solution.py:540
  33.2 1.4 %copy-done.22 = f32[256,2048]{1,0:T(8,128)} copy-done((f32[256,2048]{1,0:T(8,128)}, f32[256,2048]{1,0:T(8,128)S(1)}, u32[]{:S(2)}) %copy-start.22) | copy-done | bytes 2097176
  34.6 0.0 collective-permute-done.4.refs_5_
  34.6 0.0 collective-permute-done.refs_2_
  34.6 0.0 copy-start.8
  34.7 0.0 copy-start.21
  34.7 7.4 %scores.1 = (bf16[128,2048]{1,0:T(8,128)(2,1)S(1)}, f32[256,2048]{1,0:T(8,128)}, bf16[256,2048]{1,0:T(8,128)(2,1)S(1)}, f32[8,128]{1,0:T(8,128)S(1)}) custom-call(s32[8]{0:T(128)S(1)} %copy-done.12, bf16[3,128,2048]{2,1,0:T(8,128)(2,1)S(1)} %copy-done.1, bf16[128,2048]{1,0:T(8,128)(2,1)S(1)} %collective-permute-done.refs_2_, f32[3,7,2048]{2,1,0:T(8,128)S(1)} %copy-done.7, ...), custom_call_target="tpu_custom_call" | custom-call | flops 3000000000 | bytes 9000000 | tf_op jit(solution)/shard_map/scores/pallas_call | solution.py:555
  42.0 1.0 copy-done.2
  43.0 0.8 copy-done.17
  43.9 0.0 collective-permute-start.6
  43.9 1.2 %collective-permute-done.6 = f32[8,128]{1,0:T(8,128)S(1)} collective-permute-done((f32[8,128]{1,0:T(8,128)S(1)}, f32[8,128]{1,0:T(8,128)S(1)}, u32[]{:S(2)}, u32[]{:S(2)}) %collective-permute-start.6) | collective-permute-done | bytes 4128 | tf_op jit(solution)/shard_map/ppermute | solution.py:26
  45.0 1.5 %collective-permute-start.7 = (f32[8,128]{1,0:T(8,128)S(1)}, f32[8,128]{1,0:T(8,128)S(1)}, u32[]{:S(2)}, u32[]{:S(2)}) collective-permute-start(f32[8,128]{1,0:T(8,128)S(1)} %add.12), channel_id=1, source_target_pairs={{0,2},{2,0},{1,3},{3,1},{4,6},{6,4},{5,7},{7,5},{8,10},{10,8},{9,1... | collective-permute-start | bytes 12296 | tf_op jit(solution)/shard_map/ppermute | solution.py:26
  46.5 2.1 %collective-permute-done.7 = f32[8,128]{1,0:T(8,128)S(1)} collective-permute-done((f32[8,128]{1,0:T(8,128)S(1)}, f32[8,128]{1,0:T(8,128)S(1)}, u32[]{:S(2)}, u32[]{:S(2)}) %collective-permute-start.7) | collective-permute-done | bytes 4128 | tf_op jit(solution)/shard_map/ppermute | solution.py:26
  48.6 1.3 %collective-permute-start.10 = (bf16[128,2048]{1,0:T(8,128)(2,1)S(1)}, bf16[128,2048]{1,0:T(8,128)(2,1)S(1)}, u32[]{:S(2)}, u32[]{:S(2)}) collective-permute-start(bf16[128,2048]{1,0:T(8,128)(2,1)S(1)} %get-tuple-element.32.refs_1_.refs_6_), channel_id=1, source_target_pairs={{0,1},{1,4},{4,5},{5,8},{8,9},{9,12},{12,13},{2,3},{3,6},{6,7},{7,... | collective-permute-start | bytes 1572872 | tf_op jit(solution)/shard_map/ppermute | solution.py:21
  50.0 2.4 %collective-permute-done.8 = f32[8,128]{1,0:T(8,128)} collective-permute-done((f32[8,128]{1,0:T(8,128)S(1)}, f32[8,128]{1,0:T(8,128)}, u32[]{:S(2)}, u32[]{:S(2)}) %collective-permute-start.8) | collective-permute-done | bytes 4128 | tf_op jit(solution)/shard_map/ppermute | solution.py:26
  52.3 0.7 add.14
  53.0 1.2 %collective-permute-start.9 = (f32[8,128]{1,0:T(8,128)S(1)}, f32[8,128]{1,0:T(8,128)S(1)}, u32[]{:S(2)}, u32[]{:S(2)}) collective-permute-start(f32[8,128]{1,0:T(8,128)S(1)} %add.14), channel_id=1, source_target_pairs={{0,8},{4,12},{8,0},{12,4},{1,9},{5,13},{9,1},{13,5},{2,10},{6,14},... | collective-permute-start | bytes 12296 | tf_op jit(solution)/shard_map/ppermute | solution.py:26
  54.2 1.6 %copy-done.14 = f32[256,2048]{1,0:T(8,128)S(1)} copy-done((f32[256,2048]{1,0:T(8,128)S(1)}, f32[256,2048]{1,0:T(8,128)}, u32[]{:S(2)}) %copy-start.14) | copy-done | bytes 2097176
  55.8 1.0 copy-done.18
  56.9 8.0 %adjoint_of_q.1.refs_13_ = f32[128,2048]{1,0:T(8,128)S(1)} custom-call(s32[8]{0:T(128)S(1)} %copy-done.12, bf16[128,2048]{1,0:T(8,128)(2,1)S(1)} %get-tuple-element.33.refs_2_.refs_1_.refs_6_, bf16[128,2048]{1,0:T(8,128)(2,1)S(1)} %copy-done.18, f32[256,2048]{1,0:T(8,128)S(1)} %copy-done.14, f32[256,256]{1,0:T(8,128)S(1)} %copy-done.21, f32[128,256]{1,0:T(8,128)S(1)} %copy-done.8), custom_call_target="tpu_custom_call" | custom-call | flops 3000000000 | bytes 9000000 | tf_op jit(solution)/shard_map/adjoint_of_q/pallas_call | solution.py:568
  64.9 1.0 copy-done.3
  65.9 0.0 collective-permute-done.9
  65.9 0.0 collective-permute-done.11.refs_4_
  65.9 0.0 copy-start.20
  65.9 11.2 %adjoint_of_up.1 = (f32[128,2048]{1,0:T(8,128)S(1)}, f32[256,2048]{1,0:T(8,128)}) custom-call(s32[8]{0:T(128)S(1)} %copy-done.12, bf16[128,2048]{1,0:T(8,128)(2,1)S(1)} %get-tuple-element.33.refs_2_.refs_1_.refs_6_, bf16[128,2048]{1,0:T(8,128)(2,1)S(1)} %copy-done.18, bf16[128,2048]{1,0:T(8,128)(2,1)S(1)} %copy-done.4, ...), custom_call_target="tpu_custom_call" | custom-call | flops 4000000000 | bytes 12000000 | tf_op jit(solution)/shard_map/adjoint_of_up/pallas_call | solution.py:588
  77.2 8.1 %mixed.1.refs_11_ = f32[128,2048]{1,0:T(8,128)S(1)} custom-call(s32[8]{0:T(128)S(1)} %copy-done.12, bf16[128,2048]{1,0:T(8,128)(2,1)S(1)} %get-tuple-element.32.refs_1_.refs_6_, bf16[128,2048]{1,0:T(8,128)(2,1)S(1)} %collective-permute-done.10.refs_2_, f32[256,2048]{1,0:T(8,128)S(1)} %copy-done.15, f32[256,256]{1,0:T(8,128)S(1)} %copy-done.20, ...), custom_call_target="tpu_custom_call" | custom-call | flops 3000000000 | bytes 9000000 | tf_op jit(solution)/shard_map/mixed/pallas_call | solution.py:578
  85.3 10.0 %gradients.1 = (bf16[3,128,2048]{2,1,0:T(8,128)(2,1)}, bf16[3,16,2048]{2,1,0:T(8,128)(2,1)S(1)}, bf16[152,1024]{1,0:T(8,128)(2,1)S(1)}, f32[152,1024]{1,0:T(8,128)S(1)}) custom-call(s32[1]{0:T(128)} %bitcast.refs_0_, s32[8]{0:T(128)S(1)} %copy-done.12, s32[8]{0:T(128)S(1)} %copy-done.13, f32[8,128]{1,0:T(8,128)S(1)} %add.15.refs_3_, ...), custom_call_target="tpu_custom_call" | custom-call | flops 5000000000 | bytes 15000000 | tf_op jit(solution)/shard_map/gradients/pallas_call | solution.py:605
  95.3 0.1 collective-permute-start.13
  95.3 1.6 %collective-permute-done.13.recv_ref = bf16[152,1024]{1,0:T(8,128)(2,1)S(1)} collective-permute-done((bf16[152,1024]{1,0:T(8,128)(2,1)S(1)}, bf16[152,1024]{1,0:T(8,128)(2,1)S(1)}, u32[]{:S(2)}, u32[]{:S(2)}) %collective-permute-start.13) | collective-permute-done | bytes 311328 | tf_op jit(solution)/shard_map/ppermute | solution.py:26
  96.9 0.1 shares.1
  97.0 0.0 copy-start.16
  97.0 0.1 collective-permute-start.14
  97.1 0.1 collective-permute-start.15
  97.2 3.7 %collective-permute-start.16 = (bf16[56,1024]{1,0:T(8,128)(2,1)S(1)}, bf16[56,1024]{1,0:T(8,128)(2,1)S(1)}, u32[]{:S(2)}, u32[]{:S(2)}) collective-permute-start(bf16[56,1024]{1,0:T(8,128)(2,1)S(1)} %get-tuple-element.52), channel_id=1, source_target_pairs={{0,12},{4,0},{8,4},{12,8},{1,13},{5,1},{9,5},{13,9},{2,14},{6,2},{... | collective-permute-start | bytes 344072 | tf_op jit(solution)/shard_map/ppermute | solution.py:31
  100.9 1.3 %collective-permute-start.12 = (bf16[3,16,2048]{2,1,0:T(8,128)(2,1)S(1)}, bf16[3,16,2048]{2,1,0:T(8,128)(2,1)S(1)}, u32[]{:S(2)}, u32[]{:S(2)}) collective-permute-start(bf16[3,16,2048]{2,1,0:T(8,128)(2,1)S(1)} %get-tuple-element.46), channel_id=1, source_target_pairs={{1,0},{4,1},{5,4},{8,5},{9,8},{12,9},{13,12},{3,2},{6,3},{7,6},{10... | collective-permute-start | bytes 589832 | tf_op jit(solution)/shard_map/ppermute | solution.py:21
  102.2 2.8 %collective-permute-done.14.refs_0_ = bf16[56,1024]{1,0:T(8,128)(2,1)S(1)} collective-permute-done((bf16[56,1024]{1,0:T(8,128)(2,1)S(1)}, bf16[56,1024]{1,0:T(8,128)(2,1)S(1)}, u32[]{:S(2)}, u32[]{:S(2)}) %collective-permute-start.14) | collective-permute-done | bytes 114720 | tf_op jit(solution)/shard_map/ppermute | solution.py:31
  105.0 4.0 %collective-permute-done.15.refs_1_ = bf16[56,1024]{1,0:T(8,128)(2,1)S(1)} collective-permute-done((bf16[56,1024]{1,0:T(8,128)(2,1)S(1)}, bf16[56,1024]{1,0:T(8,128)(2,1)S(1)}, u32[]{:S(2)}, u32[]{:S(2)}) %collective-permute-start.15) | collective-permute-done | bytes 114720 | tf_op jit(solution)/shard_map/ppermute | solution.py:31
  108.9 0.0 collective-permute-done.16.refs_2_
  108.9 0.1 shard_sums.1.mine_ref
  109.0 0.1 collective-permute-start.17
  109.1 0.0 collective-permute-done.12.refs_2_
  109.1 4.7 %stream_grads.1 = bf16[3,128,2048]{2,1,0:T(8,128)(2,1)} custom-call(s32[8]{0:T(128)S(1)} %copy-done.12, bf16[3,128,2048]{2,1,0:T(8,128)(2,1)S(1)} %copy-done.16, bf16[3,16,2048]{2,1,0:T(8,128)(2,1)S(1)} %collective-permute-done.12.refs_2_, f32[3,7,2048]{2,1,0:T(8,128)S(1)} %copy-done.7), custom_call_target="tpu_custom_call" | custom-call | flops 4000000000 | bytes 12000000 | tf_op jit(solution)/shard_map/stream_grads/pallas_call | solution.py:629
  113.9 0.0 collective-permute-done.17.other_ref
  113.9 0.8 both_halves.1
  (35 shorter events, 0.1 us)
Async XLA Ops:
  0.6 1.4 %copy-start = (bf16[3,128,2048]{2,1,0:T(8,128)(2,1)S(1)}, bf16[3,128,2048]{2,1,0:T(8,128)(2,1)}, u32[]{:S(2)}) copy-start(bf16[3,128,2048]{2,1,0:T(8,128)(2,1)} %refs_4_.4) | copy-start | bytes 4718596
  2.0 0.9 copy-start.19
  2.9 13.4 %copy-start.4 = (bf16[128,2048]{1,0:T(8,128)(2,1)S(1)}, bf16[128,2048]{1,0:T(8,128)(2,1)}, u32[]{:S(2)}) copy-start(bf16[128,2048]{1,0:T(8,128)(2,1)} %refs_9_.3) | copy-start | bytes 1572868
  2.9 14.7 %copy-start.7 = (f32[3,7,2048]{2,1,0:T(8,128)S(1)}, f32[3,7,2048]{2,1,0:T(8,128)}, u32[]{:S(2)}) copy-start(f32[3,7,2048]{2,1,0:T(8,128)} %refs_3_.9) | copy-start | bytes 516100
  3.0 14.7 %copy-start.12 = (s32[8]{0:T(128)S(1)}, s32[8]{0:T(128)}, u32[]{:S(2)}) copy-start(s32[8]{0:T(128)} %refs_0_.13) | copy-start | bytes 100
  3.1 14.5 %collective-permute-start.5 = (bf16[3,16,2048]{2,1,0:T(8,128)(2,1)S(1)}, bf16[3,16,2048]{2,1,0:T(8,128)(2,1)S(1)}, u32[]{:S(2)}, u32[]{:S(2)}) collective-permute-start(bf16[3,16,2048]{2,1,0:T(8,128)(2,1)S(1)} %get-tuple-element.31), channel_id=1, source_target_pairs={{0,1},{1,4},{4,5},{5,8},{8,9},{9,12},{12,13},{2,3},{3,6},{6,7},{7,... | collective-permute-start | bytes 589832 | tf_op jit(solution)/shard_map/ppermute | solution.py:21
  5.6 7.9 %collective-permute-start.1 = (bf16[32,1024]{1,0:T(8,128)(2,1)S(1)}, bf16[32,1024]{1,0:T(8,128)(2,1)S(1)}, u32[]{:S(2)}, u32[]{:S(2)}) collective-permute-start(bf16[32,1024]{1,0:T(8,128)(2,1)S(1)} %get-tuple-element.30), channel_id=1, source_target_pairs={{0,4},{4,8},{8,12},{12,0},{1,5},{5,9},{9,13},{13,1},{2,6},{6,10},{... | collective-permute-start | bytes 196616 | tf_op jit(solution)/shard_map/ppermute | solution.py:31
  8.3 7.8 %collective-permute-start.2 = (bf16[32,1024]{1,0:T(8,128)(2,1)S(1)}, bf16[32,1024]{1,0:T(8,128)(2,1)S(1)}, u32[]{:S(2)}, u32[]{:S(2)}) collective-permute-start(bf16[32,1024]{1,0:T(8,128)(2,1)S(1)} %get-tuple-element.30), channel_id=1, source_target_pairs={{0,8},{4,12},{8,0},{12,4},{1,9},{5,13},{9,1},{13,5},{2,10},{6,14},... | collective-permute-start | bytes 196616 | tf_op jit(solution)/shard_map/ppermute | solution.py:31
  10.9 5.3 %collective-permute-start.3 = (bf16[32,1024]{1,0:T(8,128)(2,1)S(1)}, bf16[32,1024]{1,0:T(8,128)(2,1)S(1)}, u32[]{:S(2)}, u32[]{:S(2)}) collective-permute-start(bf16[32,1024]{1,0:T(8,128)(2,1)S(1)} %get-tuple-element.30), channel_id=1, source_target_pairs={{0,12},{4,0},{8,4},{12,8},{1,13},{5,1},{9,5},{13,9},{2,14},{6,2},{... | collective-permute-start | bytes 196616 | tf_op jit(solution)/shard_map/ppermute | solution.py:31
  12.2 22.4 %collective-permute-start = (bf16[128,2048]{1,0:T(8,128)(2,1)S(1)}, bf16[128,2048]{1,0:T(8,128)(2,1)S(1)}, u32[]{:S(2)}, u32[]{:S(2)}) collective-permute-start(bf16[128,2048]{1,0:T(8,128)(2,1)S(1)} %get-tuple-element.29), channel_id=1, source_target_pairs={{1,0},{4,1},{5,4},{8,5},{9,8},{12,9},{13,12},{3,2},{6,3},{7,6},{10... | collective-permute-start | bytes 1572872 | tf_op jit(solution)/shard_map/ppermute | solution.py:21
  16.2 5.8 %copy-start.9 = (f32[256,128]{1,0:T(8,128)S(1)}, f32[256,128]{1,0:T(8,128)}, u32[]{:S(2)}) copy-start(f32[256,128]{1,0:T(8,128)} %constant.16.clone.refs_4_.refs_10_.refs_9_) | copy-start | bytes 393220
  16.2 18.5 %collective-permute-start.4 = (bf16[4,32,1024]{2,1,0:T(8,128)(2,1)S(1)}, bf16[4,32,1024]{2,1,0:T(8,128)(2,1)S(1)}, u32[]{:S(2)}, u32[]{:S(2)}) collective-permute-start(bf16[4,32,1024]{2,1,0:T(8,128)(2,1)S(1)} %pad_maximum_fusion.refs_4_), channel_id=1, source_target_pairs={{0,1},{1,0},{2,3},{3,2},{4,5},{5,4},{6,7},{7,6},{8,9},{9,8},{10,11... | collective-permute-start | bytes 786440 | tf_op jit(solution)/shard_map/ppermute | solution.py:26
  16.3 49.5 %collective-permute-start.11 = (bf16[128,2048]{1,0:T(8,128)(2,1)S(1)}, bf16[128,2048]{1,0:T(8,128)(2,1)S(1)}, u32[]{:S(2)}, u32[]{:S(2)}) collective-permute-start(bf16[128,2048]{1,0:T(8,128)(2,1)S(1)} %copy-done.4), channel_id=1, source_target_pairs={{1,0},{4,1},{5,4},{8,5},{9,8},{12,9},{13,12},{3,2},{6,3},{7,6},{10... | collective-permute-start | bytes 1572872 | tf_op jit(solution)/shard_map/ppermute | solution.py:21
  22.0 11.2 %copy-start.5 = (bf16[128,2048]{1,0:T(8,128)(2,1)}, bf16[128,2048]{1,0:T(8,128)(2,1)S(1)}, u32[]{:S(2)}) copy-start(bf16[128,2048]{1,0:T(8,128)(2,1)S(1)} %get-tuple-element.37.refs_8_) | copy-start | bytes 1572868
  22.0 12.6 %copy-start.1 = (bf16[3,128,2048]{2,1,0:T(8,128)(2,1)S(1)}, bf16[3,128,2048]{2,1,0:T(8,128)(2,1)}, u32[]{:S(2)}) copy-start(bf16[3,128,2048]{2,1,0:T(8,128)(2,1)} %refs_4_.4) | copy-start | bytes 4718596
  22.0 12.6 %copy-start.10 = (f32[256,128]{1,0:T(8,128)S(1)}, f32[256,128]{1,0:T(8,128)}, u32[]{:S(2)}) copy-start(f32[256,128]{1,0:T(8,128)} %constant.18.clone.refs_9_) | copy-start | bytes 393220
  22.0 12.6 %copy-start.11 = (f32[2048]{0:T(1024)S(1)}, f32[2048]{0:T(1024)}, u32[]{:S(2)}) copy-start(f32[2048]{0:T(1024)} %param.16) | copy-start | bytes 24580
  33.2 1.4 %copy-start.22 = (f32[256,2048]{1,0:T(8,128)}, f32[256,2048]{1,0:T(8,128)S(1)}, u32[]{:S(2)}) copy-start(f32[256,2048]{1,0:T(8,128)S(1)} %get-tuple-element.41.refs_7_) | copy-start | bytes 6291460
  34.6 19.6 %copy-start.8 = (f32[128,256]{1,0:T(8,128)S(1)}, f32[128,256]{1,0:T(8,128)}, u32[]{:S(2)}) copy-start(f32[128,256]{1,0:T(8,128)} %constant.17.clone.refs_5_.refs_10_.refs_17_) | copy-start | bytes 393220
  34.7 19.6 %copy-start.21 = (f32[256,256]{1,0:T(8,128)S(1)}, f32[256,256]{1,0:T(8,128)}, u32[]{:S(2)}) copy-start(f32[256,256]{1,0:T(8,128)} %constant.14.clone.refs_8_.refs_4_) | copy-start | bytes 786436
  42.0 1.0 copy-start.2
  43.0 0.8 copy-start.17
  43.9 1.2 %collective-permute-start.6 = (f32[8,128]{1,0:T(8,128)S(1)}, f32[8,128]{1,0:T(8,128)S(1)}, u32[]{:S(2)}, u32[]{:S(2)}) collective-permute-start(f32[8,128]{1,0:T(8,128)S(1)} %get-tuple-element.35), channel_id=1, source_target_pairs={{0,1},{1,0},{2,3},{3,2},{4,5},{5,4},{6,7},{7,6},{8,9},{9,8},{10,11... | collective-permute-start | bytes 12296 | tf_op jit(solution)/shard_map/ppermute | solution.py:26
  45.0 3.6 %collective-permute-start.7 = (f32[8,128]{1,0:T(8,128)S(1)}, f32[8,128]{1,0:T(8,128)S(1)}, u32[]{:S(2)}, u32[]{:S(2)}) collective-permute-start(f32[8,128]{1,0:T(8,128)S(1)} %add.12), channel_id=1, source_target_pairs={{0,2},{2,0},{1,3},{3,1},{4,6},{6,4},{5,7},{7,5},{8,10},{10,8},{9,1... | collective-permute-start | bytes 12296 | tf_op jit(solution)/shard_map/ppermute | solution.py:26
  48.6 3.7 %collective-permute-start.8 = (f32[8,128]{1,0:T(8,128)S(1)}, f32[8,128]{1,0:T(8,128)}, u32[]{:S(2)}, u32[]{:S(2)}) collective-permute-start(f32[8,128]{1,0:T(8,128)S(1)} %add.13), channel_id=1, source_target_pairs={{0,4},{4,0},{8,12},{12,8},{1,5},{5,1},{9,13},{13,9},{2,6},{6,2},{1... | collective-permute-start | bytes 12296 | tf_op jit(solution)/shard_map/ppermute | solution.py:26
  48.6 28.5 %collective-permute-start.10 = (bf16[128,2048]{1,0:T(8,128)(2,1)S(1)}, bf16[128,2048]{1,0:T(8,128)(2,1)S(1)}, u32[]{:S(2)}, u32[]{:S(2)}) collective-permute-start(bf16[128,2048]{1,0:T(8,128)(2,1)S(1)} %get-tuple-element.32.refs_1_.refs_6_), channel_id=1, source_target_pairs={{0,1},{1,4},{4,5},{5,8},{8,9},{9,12},{12,13},{2,3},{3,6},{6,7},{7,... | collective-permute-start | bytes 1572872 | tf_op jit(solution)/shard_map/ppermute | solution.py:21
  53.0 12.9 %collective-permute-start.9 = (f32[8,128]{1,0:T(8,128)S(1)}, f32[8,128]{1,0:T(8,128)S(1)}, u32[]{:S(2)}, u32[]{:S(2)}) collective-permute-start(f32[8,128]{1,0:T(8,128)S(1)} %add.14), channel_id=1, source_target_pairs={{0,8},{4,12},{8,0},{12,4},{1,9},{5,13},{9,1},{13,5},{2,10},{6,14},... | collective-permute-start | bytes 12296 | tf_op jit(solution)/shard_map/ppermute | solution.py:26
  54.2 1.6 %copy-start.14 = (f32[256,2048]{1,0:T(8,128)S(1)}, f32[256,2048]{1,0:T(8,128)}, u32[]{:S(2)}) copy-start(f32[256,2048]{1,0:T(8,128)} %get-tuple-element.38.refs_3_.refs_5_) | copy-start | bytes 6291460
  55.8 1.0 copy-start.18
  64.9 1.0 copy-start.3
  65.9 11.2 %copy-start.15 = (f32[256,2048]{1,0:T(8,128)S(1)}, f32[256,2048]{1,0:T(8,128)}, u32[]{:S(2)}) copy-start(f32[256,2048]{1,0:T(8,128)} %get-tuple-element.38.refs_3_.refs_5_) | copy-start | bytes 6291460
  65.9 11.2 %copy-start.20 = (f32[256,256]{1,0:T(8,128)S(1)}, f32[256,256]{1,0:T(8,128)}, u32[]{:S(2)}) copy-start(f32[256,256]{1,0:T(8,128)} %constant.15.clone.refs_4_) | copy-start | bytes 786436
  77.1 8.1 %copy-start.6 = (bf16[128,2048]{1,0:T(8,128)(2,1)S(1)}, bf16[128,2048]{1,0:T(8,128)(2,1)}, u32[]{:S(2)}) copy-start(bf16[128,2048]{1,0:T(8,128)(2,1)} %copy-done.5) | copy-start | bytes 1572868
  77.1 8.1 %copy-start.13 = (s32[8]{0:T(128)S(1)}, s32[8]{0:T(128)}, u32[]{:S(2)}) copy-start(s32[8]{0:T(128)} %refs_2_.1) | copy-start | bytes 100
  95.3 1.7 %collective-permute-start.13 = (bf16[152,1024]{1,0:T(8,128)(2,1)S(1)}, bf16[152,1024]{1,0:T(8,128)(2,1)S(1)}, u32[]{:S(2)}, u32[]{:S(2)}) collective-permute-start(bf16[152,1024]{1,0:T(8,128)(2,1)S(1)} %get-tuple-element.48), channel_id=1, source_target_pairs={{0,1},{1,0},{2,3},{3,2},{4,5},{5,4},{6,7},{7,6},{8,9},{9,8},{10,11... | collective-permute-start | bytes 933896 | tf_op jit(solution)/shard_map/ppermute | solution.py:26
  97.0 12.1 %copy-start.16 = (bf16[3,128,2048]{2,1,0:T(8,128)(2,1)S(1)}, bf16[3,128,2048]{2,1,0:T(8,128)(2,1)}, u32[]{:S(2)}) copy-start(bf16[3,128,2048]{2,1,0:T(8,128)(2,1)} %get-tuple-element.45.refs_1_) | copy-start | bytes 4718596
  97.0 7.9 %collective-permute-start.14 = (bf16[56,1024]{1,0:T(8,128)(2,1)S(1)}, bf16[56,1024]{1,0:T(8,128)(2,1)S(1)}, u32[]{:S(2)}, u32[]{:S(2)}) collective-permute-start(bf16[56,1024]{1,0:T(8,128)(2,1)S(1)} %get-tuple-element.50), channel_id=1, source_target_pairs={{0,4},{4,8},{8,12},{12,0},{1,5},{5,9},{9,13},{13,1},{2,6},{6,10},{... | collective-permute-start | bytes 344072 | tf_op jit(solution)/shard_map/ppermute | solution.py:31
  97.1 11.9 %collective-permute-start.15 = (bf16[56,1024]{1,0:T(8,128)(2,1)S(1)}, bf16[56,1024]{1,0:T(8,128)(2,1)S(1)}, u32[]{:S(2)}, u32[]{:S(2)}) collective-permute-start(bf16[56,1024]{1,0:T(8,128)(2,1)S(1)} %get-tuple-element.51), channel_id=1, source_target_pairs={{0,8},{4,12},{8,0},{12,4},{1,9},{5,13},{9,1},{13,5},{2,10},{6,14},... | collective-permute-start | bytes 344072 | tf_op jit(solution)/shard_map/ppermute | solution.py:31
  97.2 11.8 %collective-permute-start.16 = (bf16[56,1024]{1,0:T(8,128)(2,1)S(1)}, bf16[56,1024]{1,0:T(8,128)(2,1)S(1)}, u32[]{:S(2)}, u32[]{:S(2)}) collective-permute-start(bf16[56,1024]{1,0:T(8,128)(2,1)S(1)} %get-tuple-element.52), channel_id=1, source_target_pairs={{0,12},{4,0},{8,4},{12,8},{1,13},{5,1},{9,5},{13,9},{2,14},{6,2},{... | collective-permute-start | bytes 344072 | tf_op jit(solution)/shard_map/ppermute | solution.py:31
  100.9 8.2 %collective-permute-start.12 = (bf16[3,16,2048]{2,1,0:T(8,128)(2,1)S(1)}, bf16[3,16,2048]{2,1,0:T(8,128)(2,1)S(1)}, u32[]{:S(2)}, u32[]{:S(2)}) collective-permute-start(bf16[3,16,2048]{2,1,0:T(8,128)(2,1)S(1)} %get-tuple-element.46), channel_id=1, source_target_pairs={{1,0},{4,1},{5,4},{8,5},{9,8},{12,9},{13,12},{3,2},{6,3},{7,6},{10... | collective-permute-start | bytes 589832 | tf_op jit(solution)/shard_map/ppermute | solution.py:21
  109.0 4.8 %collective-permute-start.17 = (f32[56,1024]{1,0:T(8,128)S(1)}, f32[56,1024]{1,0:T(8,128)S(1)}, u32[]{:S(2)}, u32[]{:S(2)}) collective-permute-start(f32[56,1024]{1,0:T(8,128)S(1)} %shard_sums.1.mine_ref), channel_id=1, source_target_pairs={{0,1},{1,0},{2,3},{3,2},{4,5},{5,4},{6,7},{7,6},{8,9},{9,8},{10,11... | collective-permute-start | bytes 688136 | tf_op jit(solution)/shard_map/ppermute | solution.py:26
